TPU v7x, 32 devices: a whole 2x2x4 slice. The times are simulated.
32 devices in a mesh: row: 16 (over z, y, core), col: 2 (over x).
Axes of the slice: x: 2, y: 2, z: 4, core: 2. Of those that a mesh axis runs over, the one named last changes fastest.
Arguments:
- pair: bfloat16 [64, 128, 128], P(None, 'row', 'col'), may hold values from -18 to 18
- dilations: int32 [2], replicated, may hold values from 1 to 4, as said below
- mask: int32 [128], replicated, may hold values from 0 to 1, as said below
- labels: int32 [128, 128], P('row', 'col'), may hold values from 0 to 36, as said below
- conv_first: bfloat16 [9, 64, 64], replicated, may hold values from -0.25 to 0.25
- conv_second: bfloat16 [9, 64, 64], replicated, may hold values from -0.25 to 0.25
- norm_gain: float32 [2, 64], replicated, may hold values from 0.1 to 1.9
- norm_shift: float32 [2, 64], replicated, may hold values from -3 to 3
- head_weight: bfloat16 [64, 37], replicated, may hold values from -25 to 25
- head_bias: float32 [37], replicated, may hold values from -4 to 4
Outputs:
- loss: float32 [], replicated
- grad_head: float32 [64, 37], replicated
- grad_bias: float32 [37], replicated
- grad_norm: float32 [2, 64], replicated
- grad_conv: float32 [9, 64, 64], replicated
- act_grad: bfloat16 [64, 128, 128], P(None, 'row', 'col')
Inputs may be any that keep to these rules, and one draw needn't show every extreme that they name: `dilations`: one of the two entries is 4. `mask`: residue 0 is valid. labels[i, j] == labels[j, i].
All inputs are finite; a program needn't handle non-finite values.
Results may differ from a plain program's by a relative error of at most 0.0094.
Values may be sent and summed in bfloat16 or wider, within the bound.
A program may use at most 64 MiB of HBM per device.

v0:
```python
import jax
import jax.numpy as jnp
from jax import lax
from jax.sharding import PartitionSpec as P

DMAX = 4


EPSILON = 1e-05


def with_halo(value, sides, width):
    for axis, dim in sides:
        devices, length = (lax.axis_size(axis), value.shape[dim])
        up = [(i, (i + 1) % devices) for i in range(devices - 1)]
        down = [(j, i) for i, j in up]
        last = lax.slice_in_dim(value, length - width, length, axis=dim)
        initial = lax.slice_in_dim(value, 0, width, axis=dim)
        before = lax.ppermute(last, axis, up)
        after = lax.ppermute(initial, axis, down)
        value = jnp.concatenate([before, value, after], axis=dim)
    return value


def with_rim(field_tile):
    return with_halo(field_tile, (("row", 1), ("col", 2)), DMAX)


def dilated(padded, weight, dilation, direction, row_count, col_count):
    in_chans = padded.shape[0]
    accumulated = None
    for tap_index in range(9):
        offset_down = tap_index // 3 - 1
        offset_right = tap_index % 3 - 1
        start_at = (
            jnp.int32(0),
            DMAX + direction * offset_down * dilation,
            DMAX + direction * offset_right * dilation,
        )
        window_piece = lax.dynamic_slice(padded, start_at, (in_chans, row_count, col_count))
        kernel = weight[tap_index] if direction > 0 else weight[tap_index].T
        contribution = jnp.dot(
            kernel,
            window_piece.reshape(in_chans, row_count * col_count),
            preferred_element_type=jnp.float32,
        )
        accumulated = contribution if accumulated is None else accumulated + contribution
    return accumulated.reshape(-1, row_count, col_count)


def kernel_grad(padded, upstream, dilation, row_count, col_count):
    in_chans = padded.shape[0]
    flat_up = upstream.reshape(upstream.shape[0], row_count * col_count)
    tap_terms = []
    for tap_index in range(9):
        offset_down = tap_index // 3 - 1
        offset_right = tap_index % 3 - 1
        start_at = (jnp.int32(0), DMAX + offset_down * dilation, DMAX + offset_right * dilation)
        window_piece = lax.dynamic_slice(padded, start_at, (in_chans, row_count, col_count))
        tap_terms.append(
            lax.dot_general(
                flat_up,
                window_piece.reshape(in_chans, row_count * col_count),
                (((1,), (1,)), ((), ())),
                preferred_element_type=jnp.float32,
            )
        )
    return jnp.stack(tap_terms)


def moments(hidden, pair_mask, count):
    masked = pair_mask[None] * hidden
    first_sum, square_sum = lax.psum(
        (jnp.sum(masked, axis=(1, 2)), jnp.sum(masked * hidden, axis=(1, 2))), ("row", "col")
    )
    mean_value = first_sum / count
    variance = square_sum / count - mean_value * mean_value
    return (mean_value, variance)


def split_mirror(tile_part):
    bin_count, row_count, col_count = tile_part.shape
    row_devices = lax.axis_size("row")
    row_ratio = row_devices // lax.axis_size("col")
    piece_width = row_count * row_count // row_devices
    pieces = tile_part.reshape(bin_count, row_count, row_ratio, row_count).transpose(0, 2, 3, 1)
    return pieces.reshape(bin_count, row_ratio, row_devices, piece_width).transpose(0, 2, 1, 3)


def regroup_cols(section_one):
    bin_count, row_devices, row_ratio, piece_width = section_one.shape
    col_devices = row_devices // row_ratio
    regrouped = section_one.reshape(bin_count, col_devices, row_ratio, row_ratio, piece_width)
    return regrouped.transpose(0, 1, 3, 2, 4)


def regroup_rows(section_two):
    bin_count, col_devices, row_ratio, ratio_again, piece_width = section_two.shape
    return section_two.reshape(bin_count, col_devices * row_ratio, ratio_again, piece_width)


def join_mirror(section_three, row_count, col_count):
    bin_count, row_devices, row_ratio, piece_width = section_three.shape
    joined = section_three.transpose(0, 2, 1, 3).reshape(bin_count, row_ratio, row_count, row_count)
    return joined.transpose(0, 2, 1, 3).reshape(bin_count, row_count, col_count)


def mirror_logits(tile_part):
    section_one = lax.all_to_all(
        split_mirror(tile_part), "row", split_axis=1, concat_axis=1, tiled=True
    )
    section_two = lax.all_to_all(
        regroup_cols(section_one), "col", split_axis=1, concat_axis=1, tiled=True
    )
    section_three = lax.all_to_all(
        regroup_rows(section_two), "row", split_axis=1, concat_axis=1, tiled=True
    )
    return join_mirror(section_three, tile_part.shape[1], tile_part.shape[2])


def apply_head(head_weight, flat_features):
    return lax.dot_general(
        head_weight, flat_features, (((0,), (0,)), ((), ())), preferred_element_type=jnp.float32
    )


def body(
    pair,
    dilations,
    mask,
    labels,
    conv_first,
    conv_second,
    norm_gain,
    norm_shift,
    head_weight,
    head_bias,
):
    channels, row_count, col_count = pair.shape
    bin_count = head_weight.shape[1]
    cell_count = row_count * col_count
    extent = row_count * lax.axis_size("row")
    mask_float = mask.astype(jnp.float32)
    valid_total = jnp.sum(mask_float)
    count = valid_total * valid_total
    row_mask = lax.dynamic_slice_in_dim(mask_float, lax.axis_index("row") * row_count, row_count)
    col_mask = lax.dynamic_slice_in_dim(mask_float, lax.axis_index("col") * col_count, col_count)
    pair_mask = row_mask[:, None] * col_mask[None, :]
    first_rate = dilations[0]
    second_rate = dilations[1]
    hidden_one = dilated(with_rim(pair), conv_first, first_rate, 1, row_count, col_count)
    mean_one, var_one = moments(hidden_one, pair_mask, count)
    normed_one = (
        norm_gain[0][:, None, None]
        * (hidden_one - mean_one[:, None, None])
        / jnp.sqrt(var_one + EPSILON)[:, None, None]
        + norm_shift[0][:, None, None]
    )
    activation = (pair_mask[None] * jax.nn.elu(normed_one)).astype(jnp.bfloat16)
    padded_act = with_rim(activation)
    hidden_two = dilated(padded_act, conv_second, second_rate, 1, row_count, col_count)
    mean_two, var_two = moments(hidden_two, pair_mask, count)
    inverse_two = 1.0 / jnp.sqrt(var_two + EPSILON)
    normal_two = (hidden_two - mean_two[:, None, None]) * inverse_two[:, None, None]
    summed = (
        norm_gain[1][:, None, None] * normal_two
        + norm_shift[1][:, None, None]
        + pair.astype(jnp.float32)
    )
    output = (pair_mask[None] * jax.nn.elu(summed)).astype(jnp.bfloat16)
    flat_out = output.reshape(channels, cell_count)
    logits = (apply_head(head_weight, flat_out) + head_bias[:, None]).reshape(
        bin_count, row_count, col_count
    )
    scores = 0.5 * (logits + mirror_logits(logits))
    top_score = jnp.max(scores, axis=0)
    log_total = top_score + jnp.log(jnp.sum(jnp.exp(scores - top_score[None]), axis=0))
    one_hot = (labels[None, :, :] == jnp.arange(bin_count, dtype=jnp.int32)[:, None, None]).astype(
        jnp.float32
    )
    picked = jnp.sum(one_hot * scores, axis=0)
    loss_local = jnp.sum(pair_mask * (log_total - picked))
    logit_grad = pair_mask[None] * (jnp.exp(scores - log_total[None]) - one_hot)
    logit_half = logit_grad.astype(jnp.bfloat16).reshape(bin_count, cell_count)
    head_local = lax.dot_general(
        flat_out, logit_half, (((1,), (1,)), ((), ())), preferred_element_type=jnp.float32
    )
    output_grad = jnp.dot(head_weight, logit_half, preferred_element_type=jnp.float32).reshape(
        channels, row_count, col_count
    )
    summed_grad = (
        output_grad
        * pair_mask[None]
        * jnp.where(summed > 0, 1.0, jnp.exp(jnp.minimum(summed, 0.0)))
    )
    head_sum, bias_sum, loss_sum, scale_sum, shift_sum = lax.psum(
        (
            head_local,
            jnp.sum(logit_grad, axis=(1, 2)),
            loss_local,
            jnp.sum(summed_grad * normal_two, axis=(1, 2)),
            jnp.sum(summed_grad, axis=(1, 2)),
        ),
        ("row", "col"),
    )
    pre_grad = (
        pair_mask[None]
        * (norm_gain[1] * inverse_two)[:, None, None]
        * (
            summed_grad
            - (shift_sum / count)[:, None, None]
            - normal_two * (scale_sum / count)[:, None, None]
        )
    )
    pre_half = pre_grad.astype(jnp.bfloat16)
    act_grad = dilated(
        with_rim(pre_half), conv_second, second_rate, -1, row_count, col_count
    ).astype(jnp.bfloat16)
    kernel_local = kernel_grad(padded_act, pre_half, second_rate, row_count, col_count)
    kernel_sum = lax.psum(kernel_local, ("row", "col"))
    return (
        loss_sum / count,
        head_sum / extent,
        bias_sum / extent,
        jnp.stack([scale_sum, shift_sum]) / extent,
        kernel_sum / extent,
        act_grad,
    )


def solution(mesh):
    placed = (P(None, "row", "col"), P(), P(), P("row", "col"), P(), P(), P(), P(), P(), P())
    return jax.shard_map(
        body,
        mesh=mesh,
        in_specs=placed,
        out_specs=(P(), P(), P(), P(), P(), P(None, "row", "col")),
        check_vma=False,
    )
```

profile of v0, /device:TPU:0, one launch (start us, length us, event | category | flops | bytes accessed | tf_op | source)
XLA Modules:
  0.0 369.8 jit_solution(3432956156395832376)
XLA Ops:
  7.2 1.1 fusion.128
  8.3 1.4 collective-permute-start.1
  9.7 3.0 collective-permute-start
  16.6 1.3 collective-permute-start.3
  17.9 4.9 %collective-permute-start.2 = (bf16[64,16,4]{2,1,0:T(8,128)(2,1)S(1)}, bf16[64,16,4]{2,1,0:T(8,128)(2,1)S(1)}, u32[]{:S(2)}, u32[]{:S(2)}) collective-permute-start(bf16[64,16,4]{2,1,0:T(8,128)(2,1)S(1)} %get-tuple-element.59), channel_id=1, source_target_pairs={{0,1},{2,3},{4,5},{6,7},{8,9},{10,11},{12,13},{14,15},{16,17},{18,... | collective-permute-start | bytes 24584 | tf_op jit(solution)/shard_map/ppermute | solution.py:19
  31.9 43.0 %all-reduce.2 = (f32[64]{0:T(128)S(1)}, f32[64]{0:T(128)S(1)}) all-reduce(f32[64]{0:T(128)S(1)} %get-tuple-element.11, f32[64]{0:T(128)S(1)} %get-tuple-element.10), channel_id=1, replica_groups=mesh['row'=16,'col'=2] {'row','col'}, use_global_device_ids=true, to_apply=%region_1.0 | all-reduce | flops 128 | bytes 1024 | tf_op jit(solution)/shard_map/psum | solution.py:73
  75.2 1.3 collective-permute-start.5
  76.5 3.0 collective-permute-start.4
  79.6 0.9 collective-permute-done.4
  80.7 1.3 collective-permute-start.7
  82.0 4.6 %collective-permute-start.6 = (bf16[64,16,4]{2,0,1:T(8,128)(2,1)S(1)}, bf16[64,16,4]{2,0,1:T(8,128)(2,1)S(1)}, u32[]{:S(2)}, u32[]{:S(2)}) collective-permute-start(bf16[64,16,4]{2,0,1:T(8,128)(2,1)S(1)} %get-tuple-element.49), channel_id=1, source_target_pairs={{0,1},{2,3},{4,5},{6,7},{8,9},{10,11},{12,13},{14,15},{16,17},{18,... | collective-permute-start | bytes 24584 | tf_op jit(solution)/shard_map/ppermute | solution.py:19
  89.1 1.2 collective-permute-done.7
  90.3 1.8 collective-permute-done.6
  97.2 43.1 %all-reduce.1 = (f32[64]{0:T(128)S(1)}, f32[64]{0:T(128)S(1)}) all-reduce(f32[64]{0:T(128)S(1)} %get-tuple-element.9, f32[64]{0:T(128)S(1)} %get-tuple-element.8), channel_id=1, replica_groups=mesh['row'=16,'col'=2] {'row','col'}, use_global_device_ids=true, to_apply=%region_6.7 | all-reduce | flops 128 | bytes 1024 | tf_op jit(solution)/shard_map/psum | solution.py:73
  141.9 12.3 %all_to_all.15 = f32[16,1,1184]{2,1,0:T(1,128)S(1)} all-to-all(f32[16,1,1184]{2,1,0:T(1,128)S(1)} %reshape.317), channel_id=1, replica_groups=mesh['row'=16,'col'=2] {'row'}, dimensions={0} | all-to-all | bytes 151552 | tf_op jit(solution)/shard_map/all_to_all | solution.py:109
  154.8 0.8 reduce.16
  156.4 6.5 %all_to_all.16 = f32[2,1,9472]{2,1,0:T(1,128)S(1)} all-to-all(f32[2,1,9472]{2,1,0:T(1,128)S(1)} %reshape.319), channel_id=1, replica_groups=mesh['row'=16,'col'=2] {'col'}, dimensions={0} | all-to-all | bytes 151552 | tf_op jit(solution)/shard_map/all_to_all | solution.py:112
  162.9 0.9 reduce.17
  164.0 0.9 reshape.321
  164.9 3.6 all-to-all-start.2
  168.9 6.8 %all-to-all-done.2 = f32[16,1,1184]{2,1,0:T(1,128)S(1)} async-done(((f32[16,1,1184]{2,1,0:T(1,128)}), f32[16,1,1184]{2,1,0:T(1,128)S(1)}, u32[]{:S(2)}, u32[]{:S(2)}) %all-to-all-start.2) | async-done | bytes 75808 | tf_op jit(solution)/shard_map/all_to_all | solution.py:115
  175.7 0.8 reduce.18
  179.2 38.2 %all-reduce = (f32[]{:T(128)}, f32[64,37]{0,1:T(8,128)S(1)}, f32[37]{0:T(128)S(1)}, f32[64]{0:T(128)S(1)}, f32[64]{0:T(128)S(1)}) all-reduce(f32[]{:T(128)} %multiply_reduce_fusion.3, f32[64,37]{0,1:T(8,128)S(1)} %convolution_bitcast_fusion.14, f32[37]{0:T(128)S(1)} %get-tuple-element.12, ...), channel_id=1, replica_groups=mesh['row'=16,'col'=2] {'row','col'}, use_global_device_ids=true, to_apply=%region_13.14 | all-reduce | flops 2534 | bytes 20272 | tf_op jit(solution)/shard_map/psum | solution.py:196
  219.8 1.3 collective-permute-start.9
  221.1 3.0 collective-permute-start.8
  225.3 1.3 collective-permute-start.11
  226.6 4.6 %collective-permute-start.10 = (bf16[64,16,4]{2,0,1:T(8,128)(2,1)S(1)}, bf16[64,16,4]{2,0,1:T(8,128)(2,1)S(1)}, u32[]{:S(2)}, u32[]{:S(2)}) collective-permute-start(bf16[64,16,4]{2,0,1:T(8,128)(2,1)S(1)} %get-tuple-element.39), channel_id=1, source_target_pairs={{0,1},{2,3},{4,5},{6,7},{8,9},{10,11},{12,13},{14,15},{16,17},{18,... | collective-permute-start | bytes 24584 | tf_op jit(solution)/shard_map/ppermute | solution.py:19
  232.6 2.5 collective-permute-done.11
  235.1 1.8 collective-permute-done.10
  241.4 0.8 convert_element_type.48
  242.2 117.9 %all-reduce.5.cloned.1.call-done = f32[9,64,64]{2,1,0:T(8,128)} async-done(((f32[9,64,64]{2,1,0:T(8,128)}), f32[9,64,64]{2,1,0:T(8,128)}) %all-reduce.5.cloned.1.call-update) | async-done | bytes 147472 | tf_op jit(solution)/shard_map/psum | solution.py:220
  360.1 1.7 broadcast_multiply_fusion
  (174 shorter events, 29.0 us)
Async XLA Ops:
  7.2 133.6 %copy-start = (bf16[64,37]{0,1:T(8,128)(2,1)S(1)}, bf16[64,37]{0,1:T(8,128)(2,1)}, u32[]{:S(2)}) copy-start(bf16[64,37]{0,1:T(8,128)(2,1)} %param.18) | copy-start | bytes 14212
  7.2 5.6 %copy-start.1 = (bf16[64,8,64]{2,1,0:T(8,128)(2,1)S(1)}, bf16[64,8,64]{2,1,0:T(8,128)(2,1)}, u32[]{:S(2)}) copy-start(bf16[64,8,64]{2,1,0:T(8,128)(2,1)} %param.10) | copy-start | bytes 196612
  8.3 6.8 %copy-start.4 = (bf16[9,64,64]{2,1,0:T(8,128)(2,1)S(1)}, bf16[9,64,64]{2,1,0:T(8,128)(2,1)}, u32[]{:S(2)}) copy-start(bf16[9,64,64]{2,1,0:T(8,128)(2,1)} %param.14) | copy-start | bytes 221188
  8.3 8.0 %collective-permute-start.1 = (bf16[64,4,64]{2,1,0:T(4,128)(2,1)S(1)}, bf16[64,4,64]{2,1,0:T(4,128)(2,1)S(1)}, u32[]{:S(2)}, u32[]{:S(2)}) collective-permute-start(bf16[64,4,64]{2,1,0:T(4,128)(2,1)S(1)} %get-tuple-element.66), channel_id=1, source_target_pairs={{2,0},{4,2},{6,4},{8,6},{10,8},{12,10},{14,12},{16,14},{18,16},{20... | collective-permute-start | bytes 98312 | tf_op jit(solution)/shard_map/ppermute | solution.py:20
  9.7 6.6 %collective-permute-start = (bf16[64,4,64]{2,1,0:T(4,128)(2,1)S(1)}, bf16[64,4,64]{2,1,0:T(4,128)(2,1)S(1)}, u32[]{:S(2)}, u32[]{:S(2)}) collective-permute-start(bf16[64,4,64]{2,1,0:T(4,128)(2,1)S(1)} %get-tuple-element.65), channel_id=1, source_target_pairs={{0,2},{2,4},{4,6},{6,8},{8,10},{10,12},{12,14},{14,16},{16,18},{18... | collective-permute-start | bytes 98312 | tf_op jit(solution)/shard_map/ppermute | solution.py:19
  12.8 0.7 copy-start.10
  13.7 0.7 copy-start.8
  14.4 0.7 copy-start.6
  15.1 0.7 copy-start.7
  16.6 11.0 %collective-permute-start.3 = (bf16[64,16,4]{2,1,0:T(8,128)(2,1)S(1)}, bf16[64,16,4]{2,1,0:T(8,128)(2,1)S(1)}, u32[]{:S(2)}, u32[]{:S(2)}) collective-permute-start(bf16[64,16,4]{2,1,0:T(8,128)(2,1)S(1)} %get-tuple-element.60), channel_id=1, source_target_pairs={{1,0},{3,2},{5,4},{7,6},{9,8},{11,10},{13,12},{15,14},{17,16},{19,... | collective-permute-start | bytes 24584 | tf_op jit(solution)/shard_map/ppermute | solution.py:20
  17.9 10.5 %collective-permute-start.2 = (bf16[64,16,4]{2,1,0:T(8,128)(2,1)S(1)}, bf16[64,16,4]{2,1,0:T(8,128)(2,1)S(1)}, u32[]{:S(2)}, u32[]{:S(2)}) collective-permute-start(bf16[64,16,4]{2,1,0:T(8,128)(2,1)S(1)} %get-tuple-element.59), channel_id=1, source_target_pairs={{0,1},{2,3},{4,5},{6,7},{8,9},{10,11},{12,13},{14,15},{16,17},{18,... | collective-permute-start | bytes 24584 | tf_op jit(solution)/shard_map/ppermute | solution.py:19
  75.2 4.3 %collective-permute-start.5 = (bf16[64,4,64]{2,0,1:T(8,128)(2,1)S(1)}, bf16[64,4,64]{2,0,1:T(8,128)(2,1)S(1)}, u32[]{:S(2)}, u32[]{:S(2)}) collective-permute-start(bf16[64,4,64]{2,0,1:T(8,128)(2,1)S(1)} %get-tuple-element.64), channel_id=1, source_target_pairs={{2,0},{4,2},{6,4},{8,6},{10,8},{12,10},{14,12},{16,14},{18,16},{20... | collective-permute-start | bytes 98312 | tf_op jit(solution)/shard_map/ppermute | solution.py:20
  76.5 3.9 %collective-permute-start.4 = (bf16[64,4,64]{2,0,1:T(8,128)(2,1)S(1)}, bf16[64,4,64]{2,0,1:T(8,128)(2,1)S(1)}, u32[]{:S(2)}, u32[]{:S(2)}) collective-permute-start(bf16[64,4,64]{2,0,1:T(8,128)(2,1)S(1)} %get-tuple-element.63), channel_id=1, source_target_pairs={{0,2},{2,4},{4,6},{6,8},{8,10},{10,12},{12,14},{14,16},{16,18},{18... | collective-permute-start | bytes 98312 | tf_op jit(solution)/shard_map/ppermute | solution.py:19
  80.7 9.7 %collective-permute-start.7 = (bf16[64,16,4]{2,0,1:T(8,128)(2,1)S(1)}, bf16[64,16,4]{2,0,1:T(8,128)(2,1)S(1)}, u32[]{:S(2)}, u32[]{:S(2)}) collective-permute-start(bf16[64,16,4]{2,0,1:T(8,128)(2,1)S(1)} %get-tuple-element.50), channel_id=1, source_target_pairs={{1,0},{3,2},{5,4},{7,6},{9,8},{11,10},{13,12},{15,14},{17,16},{19,... | collective-permute-start | bytes 24584 | tf_op jit(solution)/shard_map/ppermute | solution.py:20
  82.0 10.2 %collective-permute-start.6 = (bf16[64,16,4]{2,0,1:T(8,128)(2,1)S(1)}, bf16[64,16,4]{2,0,1:T(8,128)(2,1)S(1)}, u32[]{:S(2)}, u32[]{:S(2)}) collective-permute-start(bf16[64,16,4]{2,0,1:T(8,128)(2,1)S(1)} %get-tuple-element.49), channel_id=1, source_target_pairs={{0,1},{2,3},{4,5},{6,7},{8,9},{10,11},{12,13},{14,15},{16,17},{18,... | collective-permute-start | bytes 24584 | tf_op jit(solution)/shard_map/ppermute | solution.py:19
  93.6 0.9 copy-start.2
  140.6 0.7 copy-start.9
  164.9 3.9 %copy-start.5 = (s32[8,64]{1,0:T(8,128)S(1)}, s32[8,64]{1,0:T(8,128)}, u32[]{:S(2)}) copy-start(s32[8,64]{1,0:T(8,128)} %param.13) | copy-start | bytes 6148
  164.9 10.8 %all-to-all-start.2 = ((f32[16,1,1184]{2,1,0:T(1,128)}), f32[16,1,1184]{2,1,0:T(1,128)S(1)}, u32[]{:S(2)}, u32[]{:S(2)}) async-start(f32[16,1,1184]{2,1,0:T(1,128)} %reshape.321), calls=%async_computation.2 | async-start | bytes 163840 | tf_op jit(solution)/shard_map/all_to_all | solution.py:115
  168.6 191.6 %all-reduce.5.cloned.1.call-start = ((), (), s32[]{:S(2)}) async-start(), calls=%async_computation.3 | async-start | bytes 589824 | tf_op jit(solution)/shard_map/psum | solution.py:220
  219.8 5.4 %copy-start.3 = (f32[9,64,64]{2,1,0:T(8,128)}, f32[9,64,64]{2,1,0:T(8,128)S(1)}, u32[]{:S(2)}) copy-start(f32[9,64,64]{2,1,0:T(8,128)S(1)} %fusion.10) | copy-start | bytes 442372
  219.8 4.9 %collective-permute-start.9 = (bf16[64,4,64]{2,0,1:T(8,128)(2,1)S(1)}, bf16[64,4,64]{2,0,1:T(8,128)(2,1)S(1)}, u32[]{:S(2)}, u32[]{:S(2)}) collective-permute-start(bf16[64,4,64]{2,0,1:T(8,128)(2,1)S(1)} %get-tuple-element.62), channel_id=1, source_target_pairs={{2,0},{4,2},{6,4},{8,6},{10,8},{12,10},{14,12},{16,14},{18,16},{20... | collective-permute-start | bytes 98312 | tf_op jit(solution)/shard_map/ppermute | solution.py:20
  221.1 3.9 %collective-permute-start.8 = (bf16[64,4,64]{2,0,1:T(8,128)(2,1)S(1)}, bf16[64,4,64]{2,0,1:T(8,128)(2,1)S(1)}, u32[]{:S(2)}, u32[]{:S(2)}) collective-permute-start(bf16[64,4,64]{2,0,1:T(8,128)(2,1)S(1)} %get-tuple-element.61), channel_id=1, source_target_pairs={{0,2},{2,4},{4,6},{6,8},{8,10},{10,12},{12,14},{14,16},{16,18},{18... | collective-permute-start | bytes 98312 | tf_op jit(solution)/shard_map/ppermute | solution.py:19
  225.3 9.9 %collective-permute-start.11 = (bf16[64,16,4]{2,0,1:T(8,128)(2,1)S(1)}, bf16[64,16,4]{2,0,1:T(8,128)(2,1)S(1)}, u32[]{:S(2)}, u32[]{:S(2)}) collective-permute-start(bf16[64,16,4]{2,0,1:T(8,128)(2,1)S(1)} %get-tuple-element.40), channel_id=1, source_target_pairs={{1,0},{3,2},{5,4},{7,6},{9,8},{11,10},{13,12},{15,14},{17,16},{19,... | collective-permute-start | bytes 24584 | tf_op jit(solution)/shard_map/ppermute | solution.py:20
  226.6 10.4 %collective-permute-start.10 = (bf16[64,16,4]{2,0,1:T(8,128)(2,1)S(1)}, bf16[64,16,4]{2,0,1:T(8,128)(2,1)S(1)}, u32[]{:S(2)}, u32[]{:S(2)}) collective-permute-start(bf16[64,16,4]{2,0,1:T(8,128)(2,1)S(1)} %get-tuple-element.39), channel_id=1, source_target_pairs={{0,1},{2,3},{4,5},{6,7},{8,9},{10,11},{12,13},{14,15},{16,17},{18,... | collective-permute-start | bytes 24584 | tf_op jit(solution)/shard_map/ppermute | solution.py:19
Sparse Core Ops, SparseCore 0:
  232.6 127.4 all-reduce.4
where the time goes:
time: 371 us; the launch traced here: 370 us
  blocking collectives  143 us (39%)
  waiting for transfers between devices  134 us (36%)
  starting transfers between devices  34.9 us (9%)
  between operations  23.2 us (6%)
  local copies, waits for them, and re-layouts  17.7 us (5%)
  other arithmetic  9.95 us (3%)
  matrix products  7.04 us (2%)
    psum x1, waiting for transfers between devices, body(): kernel_sum = lax.psum(kernel_local, ('row', 'col'))  118 us
    psum x2, blocking collectives, moments(): lax.psum((jnp.sum(masked, axis=(1, 2)), jnp.sum(masked * hidden, axis=(1,...  86.1 us
    psum x1, blocking collectives, body(): lax.psum((head_local, jnp.sum(logit_grad, axis=(1, 2)), loss_local, jnp.s...  38.2 us
    ppermute x6, starting transfers between devices, with_halo(): before = lax.ppermute(last, axis, up)  23.1 us
    all_to_all x1, blocking collectives, mirror_logits(): lax.all_to_all(split_mirror(tile_part), 'row', split_axis=1, concat_axis=...  12.3 us
    ppermute x6, starting transfers between devices, with_halo(): after = lax.ppermute(initial, axis, down)  7.88 us
  transfers between devices with their start and end apart: 14, of which 9 were waited for; matrix products, arithmetic and copies ran while one was open for 2% of the time, Pallas kernels for 0%

commit v1 on v0

v1 whole, which is shorter than its diff:
```python
import functools

import jax
import jax.numpy as jnp
from jax import lax
from jax.experimental import pallas as pl
from jax.experimental.pallas import tpu as pltpu
from jax.sharding import PartitionSpec as P

EPSILON = 1e-05
LANES = 128
MESH = pl.DeviceIdType.MESH
F32 = jnp.float32
BF16 = jnp.bfloat16
NT = (((1,), (1,)), ((), ()))
DIRECTIONS = tuple((a, b) for a in (-1, 0, 1) for b in (-1, 0, 1) if (a, b) != (0, 0))


def elu(v):
    return jnp.where(v > 0, v, jnp.exp(jnp.minimum(v, 0.0)) - 1.0)


def split_of(n):
    group = 2 if n < 40 else 1
    return group, 40 // group


def kernel(
    sizes, dil, pair, rowm, colm, lab, w1, w2, par, hw, hb,
    act_out, gsum_out, tail_out,
    pb, pf, h1, a1, h2, du, dh, yb, zb, zr, zt, st1, st2, st3, part, gath, red,
    halo_s, halo_r, send_s, recv_s,
):
    R, W, C, nr, nc = sizes
    n = nr * nc
    q = W // R
    group, owners = split_of(n)
    row = lax.axis_index("row")
    col = lax.axis_index("col")
    me = row * nc + col
    my_owner = (me * owners + n - 1) // n
    is_owner = jnp.logical_and(my_owner < owners, (my_owner * n) // owners == me)

    def device(p):
        return (p // nc, p % nc)

    def to_all(slots):
        def step(k, carry):
            pltpu.make_async_remote_copy(
                src_ref=slots[0], dst_ref=slots[0], send_sem=slots[1], recv_sem=slots[2],
                device_id=device((me + k) % n), device_id_type=MESH,
            ).start()
            return carry

        lax.fori_loop(1, n, step, 0)

    def wait_bytes(ref, sem):
        pltpu.make_async_copy(ref, ref, sem).wait()

    def halo_copy(phase, index, src, src_at, dst, dst_at, width):
        dr, dc = DIRECTIONS[index]
        hr, hc = width

        def span(delta, edge, length, src_zero, dst_zero):
            if delta == 0:
                return pl.ds(src_zero, length), pl.ds(dst_zero, length)
            if delta > 0:
                return pl.ds(src_zero + length - edge, edge), pl.ds(dst_zero - edge, edge)
            return pl.ds(src_zero, edge), pl.ds(dst_zero + length, edge)

        sr, tr = span(dr, hr, R, src_at[0], dst_at[0])
        sc, tc = span(dc, hc, W, src_at[1], dst_at[1])
        return pltpu.make_async_remote_copy(
            src_ref=src.at[sr, sc, :], dst_ref=dst.at[tr, tc, :],
            send_sem=halo_s.at[phase, index], recv_sem=halo_r.at[phase, index],
            device_id=(row + dr, col + dc), device_id_type=MESH,
        )

    def inside(r, c):
        return (r >= 0) & (r < nr) & (c >= 0) & (c < nc)

    def halo_start(*spec):
        for index, (dr, dc) in enumerate(DIRECTIONS):
            @pl.when(inside(row + dr, col + dc))
            def _():
                halo_copy(spec[0], index, *spec[1:]).start()

    def halo_recv(*spec):
        for index, (dr, dc) in enumerate(DIRECTIONS):
            @pl.when(inside(row - dr, col - dc))
            def _():
                halo_copy(spec[0], index, *spec[1:]).wait_recv()

    def halo_sent(*spec):
        for index, (dr, dc) in enumerate(DIRECTIONS):
            @pl.when(inside(row + dr, col + dc))
            def _():
                halo_copy(spec[0], index, *spec[1:]).wait_send()

    def blocks(count, body):
        if count == 1:
            body(0)
        else:
            def step(k, carry):
                body(pl.multiple_of(k * 8, 8))
                return carry

            lax.fori_loop(0, count, step, 0)

    def pmask(first, lanes):
        return rowm[pl.ds(first + 4, 8), :, :lanes] * colm[8 : 8 + W, :lanes][None]

    def window(ref, r, c, cols):
        return ref[pl.ds(r, 8), pl.ds(c, cols), :].astype(BF16).reshape(8 * cols, C)

    taps = [(a, b) for a in (-1, 0, 1) for b in (-1, 0, 1)]
    inv_count = par[4:5, :]

    barrier = pltpu.get_barrier_semaphore()

    def greet(k, carry):
        pl.semaphore_signal(barrier, inc=1, device_id=device((me + k) % n), device_id_type=MESH)
        return carry

    pb[...] = jnp.zeros_like(pb)
    h2[...] = jnp.zeros_like(h2)
    du[...] = jnp.zeros_like(du)
    lax.fori_loop(1, n, greet, 0)
    pl.semaphore_wait(barrier, n - 1)

    pair_spec = (0, pair, (0, 0), pb, (8, 16), (8, 16))
    halo_start(*pair_spec)
    pb[8 : 8 + R, 16 : 16 + W, :] = pair[...]
    halo_recv(*pair_spec)
    pf[...] = pb[...].astype(F32)

    d0 = dil[0]
    d1 = dil[1]

    def first_conv(r):
        total = None
        for t, (a, b) in enumerate(taps):
            x = window(pf, r + 4 + a * d0, 8 + b * d0, W + 16)
            term = lax.dot_general(x, w1[t], NT, preferred_element_type=F32)
            total = term if total is None else total + term
        h1[pl.ds(r, 8)] = total.reshape(8, W + 16, C)

    blocks((R + 8) // 8, first_conv)

    def moments(ref, slots, phase):
        def body(first, r):
            h = ref[pl.ds(4 + r, 8), 8 : 8 + W, :]
            mh = pmask(r, C) * h
            s1 = jnp.sum(mh.reshape(8 * W, C), axis=0, keepdims=True)
            s2 = jnp.sum((mh * h).reshape(8 * W, C), axis=0, keepdims=True)
            value = jnp.concatenate([s1, s2], axis=1)
            slots[me] = value if first else slots[me] + value

        body(True, 0)
        if R > 8:
            lax.fori_loop(1, R // 8, lambda k, z: (body(False, pl.multiple_of(k * 8, 8)), z)[1], 0)
        to_all((slots.at[me], send_s.at[phase], recv_s.at[phase]))

    def gathered(slots, phase):
        wait_bytes(slots.at[pl.ds(0, n - 1)], recv_s.at[phase])
        return jnp.sum(slots[...], axis=0)

    def mean_inverse(sums):
        mean = sums[:, :C] * inv_count
        var = sums[:, C:] * inv_count - mean * mean
        return mean, 1.0 / jnp.sqrt(var + EPSILON)

    moments(h1, st1, 0)
    mean1, inv1 = mean_inverse(gathered(st1, 0))
    scale1 = par[0:1, :] * inv1
    shift1 = par[1:2, :] - mean1 * scale1

    def first_act(r):
        v = h1[pl.ds(r, 8)] * scale1[None] + shift1[None]
        m = rowm[pl.ds(r, 8), :, :C] * colm[:, :C][None]
        a1[pl.ds(r, 8)] = (m * elu(v)).astype(BF16).astype(F32)

    blocks((R + 8) // 8, first_act)

    def second_conv(r):
        total = None
        for t, (a, b) in enumerate(taps):
            x = window(a1, r + 4 + a * d1, 8 + b * d1, W)
            term = lax.dot_general(x, w2[t], NT, preferred_element_type=F32)
            total = term if total is None else total + term
        h2[pl.ds(4 + r, 8), 8 : 8 + W, :] = total.reshape(8, W, C)

    blocks(R // 8, second_conv)
    moments(h2, st2, 1)
    h2_spec = (1, h2, (4, 8), h2, (4, 8), (4, 8))
    halo_start(*h2_spec)
    mean2, inv2 = mean_inverse(gathered(st2, 1))
    gain2 = par[2:3, :]

    def features(r):
        xhat = (h2[pl.ds(4 + r, 8), 8 : 8 + W, :] - mean2[None]) * inv2[None]
        u = gain2[None] * xhat + par[3:4, :][None] + pf[pl.ds(8 + r, 8), 16 : 16 + W, :]
        return xhat, u

    def head(r):
        _, u = features(r)
        y = (pmask(r, C) * elu(u)).astype(BF16).reshape(8 * W, C)
        z = jnp.dot(y, hw[...], preferred_element_type=F32) + hb[...]
        yb[pl.ds(r, 8)] = y.reshape(8, W, C)
        zb[pl.ds(r, 8)] = z.reshape(8, W, LANES)

    blocks(R // 8, head)

    has_self = row // q == col
    mine = row % q

    def mirror_copy(b):
        return pltpu.make_async_remote_copy(
            src_ref=zb.at[:, pl.ds(b * R, R), :], dst_ref=zr.at[mine],
            send_sem=send_s.at[2], recv_sem=recv_s.at[2],
            device_id=(col * q + b, row // q), device_id_type=MESH,
        )

    for b in range(q):
        stays = has_self & (mine == b)

        @pl.when(jnp.logical_not(stays))
        def _():
            mirror_copy(b).start()

        @pl.when(stays)
        def _():
            zr[b] = zb[:, b * R : (b + 1) * R, :]

    @pl.when(has_self)
    def _():
        wait_bytes(zr.at[pl.ds(0, q - 1)], recv_s.at[2])

    @pl.when(jnp.logical_not(has_self))
    def _():
        wait_bytes(zr, recv_s.at[2])

    for b in range(q):
        zt[:, b * R : (b + 1) * R, :] = jnp.swapaxes(zr[b], 0, 1)

    def loss_part(first, r):
        s = 0.5 * (zb[pl.ds(r, 8)] + zt[pl.ds(r, 8)])
        top = jnp.max(s, axis=2, keepdims=True)
        log_total = top + jnp.log(jnp.sum(jnp.exp(s - top), axis=2, keepdims=True))
        bins = lax.broadcasted_iota(jnp.int32, (8, W, LANES), 2)
        hot = bins == lab[pl.ds(r, 8)]
        m = pmask(r, LANES)
        lossy = m * jnp.where(hot, log_total - s, 0.0)
        g = m * (jnp.exp(s - log_total) - jnp.where(hot, 1.0, 0.0))
        gh = g.astype(BF16).reshape(8 * W, LANES)
        y = yb[pl.ds(r, 8)].reshape(8 * W, C)
        head_part = jnp.dot(y.astype(F32).T.astype(BF16), gh, preferred_element_type=F32)
        dy = lax.dot_general(gh, hw[...], NT, preferred_element_type=F32).reshape(8, W, C)
        xhat, u = features(r)
        grad = dy * pmask(r, C) * jnp.where(u > 0, 1.0, jnp.exp(jnp.minimum(u, 0.0)))
        du[pl.ds(4 + r, 8), 8 : 8 + W, :] = grad
        s1 = jnp.sum((grad * xhat).reshape(8 * W, C), axis=0, keepdims=True)
        s2 = jnp.sum(grad.reshape(8 * W, C), axis=0, keepdims=True)
        bias = jnp.sum(g.reshape(8 * W, LANES), axis=0, keepdims=True)
        loss = jnp.sum(lossy.reshape(8 * W, LANES), axis=0, keepdims=True)
        value = jnp.concatenate(
            [jnp.concatenate([s1, s2], axis=1), bias, loss, jnp.zeros_like(loss)], axis=0
        )
        last = jnp.concatenate([jnp.zeros((C, C), F32), head_part[:, :C]], axis=1)
        last = last.reshape(8, 8, LANES)
        if first:
            st3[me] = value
            part[32:40] = last
        else:
            st3[me] = st3[me] + value
            part[32:40] = part[32:40] + last

    loss_part(True, 0)
    if R > 8:
        lax.fori_loop(
            1, R // 8, lambda k, z: (loss_part(False, pl.multiple_of(k * 8, 8)), z)[1], 0
        )
    to_all((st3.at[me], send_s.at[3], recv_s.at[3]))
    du_spec = (2, du, (4, 8), du, (4, 8), (4, 8))
    halo_start(*du_spec)
    halo_recv(*h2_spec)
    halo_recv(*du_spec)
    sums3 = gathered(st3, 3)
    tail_out[...] = sums3
    scale_mean = sums3[0:1, :C] * inv_count
    shift_mean = sums3[0:1, C:] * inv_count
    back = gain2 * inv2

    def second_grad(r):
        m = rowm[pl.ds(r, 8), :, :C] * colm[:, :C][None]
        xhat = (h2[pl.ds(r, 8)] - mean2[None]) * inv2[None]
        v = m * back[None] * (du[pl.ds(r, 8)] - shift_mean[None] - xhat * scale_mean[None])
        dh[pl.ds(r, 8)] = v.astype(BF16).astype(F32)

    blocks((R + 8) // 8, second_grad)

    def weight_grad(first, r):
        d = dh[pl.ds(4 + r, 8), 8 : 8 + W, :].reshape(8 * W, C)
        dt = d.T.astype(BF16)
        terms = []
        for a, b in taps:
            x = window(a1, r + 4 + a * d1, 8 + b * d1, W)
            terms.append(jnp.dot(dt, x, preferred_element_type=F32))
        terms.append(jnp.zeros((C, C), F32))
        for k in range(5):
            value = jnp.concatenate(terms[2 * k : 2 * k + 2], axis=1).reshape(8, 8, LANES)
            if first and k < 4:
                part[8 * k : 8 * k + 8] = value
            else:
                part[8 * k : 8 * k + 8] = part[8 * k : 8 * k + 8] + value

    weight_grad(True, 0)
    if R > 8:
        lax.fori_loop(
            1, R // 8, lambda k, z: (weight_grad(False, pl.multiple_of(k * 8, 8)), z)[1], 0
        )

    def scatter(k, carry):
        target = (k * n) // owners

        @pl.when(target != me)
        def _():
            pltpu.make_async_remote_copy(
                src_ref=part.at[pl.ds(k * group, group)], dst_ref=gath.at[me],
                send_sem=send_s.at[4], recv_sem=recv_s.at[4],
                device_id=device(target), device_id_type=MESH,
            ).start()

        @pl.when(target == me)
        def _():
            gath[me] = part[pl.ds(k * group, group)]

        return carry

    lax.fori_loop(0, owners, scatter, 0)

    def input_grad(r):
        total = None
        for t, (a, b) in enumerate(taps):
            x = window(dh, r + 4 - a * d1, 8 - b * d1, W)
            term = jnp.dot(x, w2[t], preferred_element_type=F32)
            total = term if total is None else total + term
        act_out[pl.ds(r, 8)] = total.reshape(8, W, C).astype(BF16)

    blocks(R // 8, input_grad)

    @pl.when(is_owner)
    def _():
        wait_bytes(gath.at[pl.ds(0, n - 1)], recv_s.at[4])
        red[pl.ds(my_owner * group, group)] = jnp.sum(gath[...], axis=0)
        mine_red = red.at[pl.ds(my_owner * group, group)]
        to_all((mine_red, send_s.at[5], recv_s.at[5]))
        wait_bytes(red.at[pl.ds(0, (owners - 1) * group)], recv_s.at[5])

    @pl.when(jnp.logical_not(is_owner))
    def _():
        wait_bytes(red, recv_s.at[5])

    gsum_out[...] = red[...]

    halo_sent(*pair_spec)
    halo_sent(*h2_spec)
    halo_sent(*du_spec)
    wait_bytes(st1.at[pl.ds(0, n - 1)], send_s.at[0])
    wait_bytes(st2.at[pl.ds(0, n - 1)], send_s.at[1])
    wait_bytes(st3.at[pl.ds(0, n - 1)], send_s.at[3])

    @pl.when(has_self)
    def _():
        wait_bytes(zr.at[pl.ds(0, q - 1)], send_s.at[2])

    @pl.when(jnp.logical_not(has_self))
    def _():
        wait_bytes(zr, send_s.at[2])

    @pl.when(is_owner)
    def _():
        wait_bytes(part.at[pl.ds(0, (owners - 1) * group)], send_s.at[4])
        wait_bytes(gath.at[pl.ds(0, n - 1)], send_s.at[5])

    @pl.when(jnp.logical_not(is_owner))
    def _():
        wait_bytes(part, send_s.at[4])


def body(
    pair, dilations, mask, labels, conv_first, conv_second,
    norm_gain, norm_shift, head_weight, head_bias,
):
    C, R, W = pair.shape
    K = head_weight.shape[1]
    nr, nc = lax.axis_size("row"), lax.axis_size("col")
    n = nr * nc
    group, owners = split_of(n)
    extent = R * nr
    mask_float = mask.astype(F32)
    valid = jnp.sum(mask_float)
    count = valid * valid
    padded = jnp.pad(mask_float, (8, 8))
    rows = lax.dynamic_slice_in_dim(padded, lax.axis_index("row") * R + 4, R + 8)
    cols = lax.dynamic_slice_in_dim(padded, lax.axis_index("col") * W, W + 16)
    rowm = jnp.broadcast_to(rows[:, None, None], (R + 8, 1, LANES))
    colm = jnp.broadcast_to(cols[:, None], (W + 16, LANES))
    par = jnp.concatenate(
        [
            jnp.stack([norm_gain[0], norm_shift[0], norm_gain[1], norm_shift[1]]),
            jnp.broadcast_to(1.0 / count, (4, C)),
        ]
    )
    hw = jnp.pad(head_weight, ((0, 0), (0, LANES - K)))
    hb = jnp.pad(head_bias[None], ((0, 0), (0, LANES - K)), constant_values=-1e30)
    vmem = pl.BlockSpec(memory_space=pltpu.VMEM)
    smem = pl.BlockSpec(memory_space=pltpu.SMEM)
    ring = (R + 8, W + 16, C)
    act, gsum, tail = pl.pallas_call(
        functools.partial(kernel, (R, W, C, nr, nc)),
        out_shape=(
            jax.ShapeDtypeStruct((R, W, C), BF16),
            jax.ShapeDtypeStruct((40, 8, LANES), F32),
            jax.ShapeDtypeStruct((4, LANES), F32),
        ),
        in_specs=[smem] + [vmem] * 9,
        out_specs=(vmem, vmem, vmem),
        scratch_shapes=[
            pltpu.VMEM((R + 16, W + 32, C), BF16),
            pltpu.VMEM((R + 16, W + 32, C), F32),
            pltpu.VMEM(ring, F32),
            pltpu.VMEM(ring, F32),
            pltpu.VMEM(ring, F32),
            pltpu.VMEM(ring, F32),
            pltpu.VMEM(ring, F32),
            pltpu.VMEM((R, W, C), BF16),
            pltpu.VMEM((R, W, LANES), F32),
            pltpu.VMEM((W // R, R, R, LANES), F32),
            pltpu.VMEM((R, W, LANES), F32),
            pltpu.VMEM((n, 1, LANES), F32),
            pltpu.VMEM((n, 1, LANES), F32),
            pltpu.VMEM((n, 4, LANES), F32),
            pltpu.VMEM((40, 8, LANES), F32),
            pltpu.VMEM((n, group, 8, LANES), F32),
            pltpu.VMEM((40, 8, LANES), F32),
            pltpu.SemaphoreType.DMA((3, 8)),
            pltpu.SemaphoreType.DMA((3, 8)),
            pltpu.SemaphoreType.DMA((6,)),
            pltpu.SemaphoreType.DMA((6,)),
        ],
        compiler_params=pltpu.CompilerParams(
            collective_id=0, has_side_effects=True, vmem_limit_bytes=56 * 1024 * 1024
        ),
    )(
        dilations, pair.transpose(1, 2, 0), rowm, colm, labels[:, :, None],
        conv_first, conv_second, par, hw, hb,
    )
    grads = gsum.reshape(5, C, 2, C).transpose(0, 2, 1, 3).reshape(10, C, C) / extent
    return (
        jnp.sum(tail[2]) / count,
        grads[9][:, :K],
        tail[1, :K] / extent,
        tail[0].reshape(2, C) / extent,
        grads[:9],
        act.transpose(2, 0, 1),
    )


def solution(mesh):
    placed = (P(None, "row", "col"), P(), P(), P("row", "col"), P(), P(), P(), P(), P(), P())
    return jax.shard_map(
        body,
        mesh=mesh,
        in_specs=placed,
        out_specs=(P(), P(), P(), P(), P(), P(None, "row", "col")),
        check_vma=False,
    )
```

time: 371 us -> 76.4 us (0.21)
  blocking collectives: 143 us -> 0 us
  waiting for transfers between devices: 134 us -> 0 us
  Pallas kernels: 0 us -> 57.5 us
  starting transfers between devices: 34.9 us -> 0 us
  between operations: 23.2 us -> 3.84 us
  local copies, waits for them, and re-layouts: 17.7 us -> 10.2 us
  matrix products: 7.04 us -> 0 us
  other arithmetic: 9.95 us -> 4.04 us
    psum x3 -> x0, blocking collectives: 124 us -> none  [the longest x2 86.1 us: moments(): lax.psum((jnp.sum(masked, axis=(1, 2)), jnp.sum(masked * hidden, axis=(1,...]
    psum x1 -> x0, waiting for transfers between devices: 118 us -> none  [body(): kernel_sum = lax.psum(kernel_local, ('row', 'col'))]
    pallas_call x0 -> x1, Pallas kernels: none -> 57.5 us  [body(): pl.pallas_call(functools.partial(kernel, (R, W, C, nr, nc)), out_shape=(j...]
    ppermute x12 -> x0, starting transfers between devices: 31 us -> none  [the longest x6 23.1 us: with_halo(): before = lax.ppermute(last, axis, up)]
    all_to_all x2 -> x0, blocking collectives: 18.8 us -> none  [the longest x1 12.3 us: mirror_logits(): lax.all_to_all(split_mirror(tile_part), 'row', split_axis=1, concat_axis=...]
    ppermute x12 -> x0, waiting for transfers between devices: 9.31 us -> none  [the longest x6 5.61 us: with_halo(): before = lax.ppermute(last, axis, up)]
    dot_general x39 -> x0, matrix products: 7.04 us -> none  [the longest x27 4.72 us: dilated(): jnp.dot(kernel, window_piece.reshape(in_chans, row_count * col_count), pr...]
    all_to_all x1 -> x0, waiting for transfers between devices: 6.79 us -> none  [mirror_logits(): lax.all_to_all(regroup_rows(section_two), 'row', split_axis=1, concat_axi...]
  transfers between devices with their start and end apart: 14 -> 0, of which waited for: 9 -> 0; matrix products, arithmetic and copies ran while one was open for 2% -> 0% of each run, Pallas kernels for 0% -> 0%
where the time goes in v1:
time: 76.4 us; the launch traced here: 75.6 us
  Pallas kernels  57.5 us (75%)
  local copies, waits for them, and re-layouts  10.2 us (13%)
  other arithmetic  4.04 us (5%)
  between operations  3.84 us (5%)
    pallas_call x1, Pallas kernels, body(): pl.pallas_call(functools.partial(kernel, (R, W, C, nr, nc)), out_shape=(j...  57.5 us
    unnamed x12, local copies, waits for them, and re-layouts  3.09 us

profile of v1, /device:TPU:0, one launch (start us, length us, event | category | flops | bytes accessed | tf_op | source)
XLA Modules:
  0.0 75.6 jit_solution(4978957548820454042)
XLA Ops:
  0.6 0.0 copy-start
  0.6 1.3 %convert_reduce_fusion = f32[]{:T(128)} fusion(s32[128]{0:T(128)} %param.12), kind=kLoop, calls=%fused_computation.7 | loop fusion | flops 255 | bytes 516 | tf_op jit(solution)/shard_map/reduce_sum | solution.py:402
  3.3 0.7 convert_element_type.7
  3.9 0.1 pad_dynamic-slice_fusion
  4.0 0.1 pad_dynamic-slice_fusion.1
  4.1 1.2 %pad.14.hb = f32[1,128]{1,0:T(1,128)} pad(f32[1,37]{1,0:T(1,128)} %bitcast.18, f32[]{:T(128)} %constant.34.clone.1), padding=0_0x0_91 | pad | bytes 664 | tf_op jit(solution)/shard_map/jit(_pad)/pad | solution.py:416
  5.3 0.8 %fusion = (f32[1,64]{1,0:T(1,128)S(1)}, f32[1,64]{1,0:T(1,128)S(1)}, f32[1,64]{1,0:T(1,128)S(1)}, f32[1,64]{1,0:T(1,128)S(1)}) fusion(f32[2,64]{1,0:T(2,128)} %param.17, f32[2,64]{1,0:T(2,128)} %param.16), kind=kLoop, calls=%fused_computation.8 | loop fusion | bytes 2048 | tf_op jit(solution)/shard_map/slice | solution.py:411
  6.0 0.6 concatenate.3.par
  6.6 0.7 broadcast_in_dim.10.rowm
  7.3 0.8 %copy.22 = bf16[64,37]{1,0:T(8,128)(2,1)S(1)} copy(bf16[64,37]{0,1:T(8,128)(2,1)} %param.18) | data formatting | bytes 9472 | tf_op args[8]
  8.1 0.6 pad.13.hw
  8.7 0.7 broadcast_in_dim.22.colm
  9.4 0.0 copy-done
  9.4 0.0 copy-start.2
  9.4 0.8 %copy.21 = bf16[64,8,64]{0,2,1:T(8,128)(2,1)} copy(bf16[64,8,64]{2,1,0:T(8,128)(2,1)S(1)} %copy-done) | data formatting | bytes 131072 | tf_op args[0]
  10.2 0.0 copy-done.2
  10.2 0.9 %copy.23.lab = s32[8,64,1]{2,1,0:T(8,128)} copy(s32[8,64,1]{1,0,2:T(8,128)S(1)} %bitcast.17) | data formatting | bytes 4096 | tf_op jit(solution)/shard_map/broadcast_in_dim | solution.py:456
  11.1 57.5 %shard_map.145 = (bf16[8,64,64]{2,1,0:T(8,128)(2,1)}, f32[40,8,128]{2,1,0:T(8,128)}, f32[4,128]{1,0:T(4,128)}) custom-call(s32[2]{0:T(128)} %dil.1, bf16[8,64,64]{2,1,0:T(8,128)(2,1)} %bitcast.14, f32[16,1,128]{2,1,0:T(1,128)} %broadcast_in_dim.10.rowm, f32[80,128]{1,0:T(8,128)} %broadcast_in_dim.22.colm, s32[8,64,1]{2,1,0:T(8,128)} %copy.23.lab, ...), custom_call_target="tpu_custom_call" | custom-call | tf_op jit(solution)/shard_map/pallas_call | solution.py:420
  68.6 0.0 copy-start.1
  68.6 1.0 %broadcast_multiply_fusion = f32[40,8,128]{2,1,0:T(8,128)S(1)} fusion(f32[40,8,128]{2,1,0:T(8,128)} %get-tuple-element.10), kind=kLoop, calls=%fused_computation | loop fusion | flops 40960 | bytes 327680 | tf_op jit(solution)/shard_map/div | solution.py:459
  69.6 0.0 copy-done.1
  69.6 0.0 copy-start.3
  69.6 0.8 %copy.26 = bf16[64,8,64]{2,1,0:T(8,128)(2,1)} copy(bf16[64,8,64]{0,2,1:T(8,128)(2,1)S(1)} %bitcast.15) | data formatting | bytes 131072
  70.4 0.0 copy-done.3
  70.4 0.5 multiply_bitcast_fusion
  70.9 0.6 multiply_reduce_fusion
  72.1 0.6 div.46
  72.8 0.2 div.38
  73.1 0.7 slice.42
  73.8 0.7 copy.25
  (3 shorter events, 0.0 us)
Async XLA Ops:
  0.6 8.8 %copy-start = (bf16[64,8,64]{2,1,0:T(8,128)(2,1)S(1)}, bf16[64,8,64]{2,1,0:T(8,128)(2,1)}, u32[]{:S(2)}) copy-start(bf16[64,8,64]{2,1,0:T(8,128)(2,1)} %param.10) | copy-start | bytes 196612
  9.4 0.8 %copy-start.2 = (s32[8,64]{1,0:T(8,128)S(1)}, s32[8,64]{1,0:T(8,128)}, u32[]{:S(2)}) copy-start(s32[8,64]{1,0:T(8,128)} %param.13) | copy-start | bytes 6148
  68.6 1.0 %copy-start.1 = (bf16[8,64,64]{2,1,0:T(8,128)(2,1)S(1)}, bf16[8,64,64]{2,1,0:T(8,128)(2,1)}, u32[]{:S(2)}) copy-start(bf16[8,64,64]{2,1,0:T(8,128)(2,1)} %get-tuple-element.11) | copy-start | bytes 196612
  69.6 0.8 %copy-start.3 = (f32[4,128]{1,0:T(4,128)S(1)}, f32[4,128]{1,0:T(4,128)}, u32[]{:S(2)}) copy-start(f32[4,128]{1,0:T(4,128)} %get-tuple-element.9) | copy-start | bytes 6148

commit v2 on v1

--- a/solution.py
+++ b/solution.py
@@ -20,21 +20,22 @@
     return jnp.where(v > 0, v, jnp.exp(jnp.minimum(v, 0.0)) - 1.0)
 
 
-def split_of(n):
-    group = 2 if n < 40 else 1
-    return group, 40 // group
+GROUP, OWNERS = 2, 20
 
 
 def kernel(
-    sizes, dil, pair, rowm, colm, lab, w1, w2, par, hw, hb,
-    act_out, gsum_out, tail_out,
-    pb, pf, h1, a1, h2, du, dh, yb, zb, zr, zt, st1, st2, st3, part, gath, red,
+    sizes, dil, mask_s, mask_v, pair, labels, w1, w2, gain, shift, head_t, bias_in,
+    act_out, grads_out, head_out, bias_out, norm_out, loss_out,
+    rowm, colm, colall, lab, hwf, hw, hw2, hb,
+    pb, pf, h1, a1, h2, du, dh, yf, zb, yp, yr, zz, zt, st1, st2, st3, part, gath, red,
     halo_s, halo_r, send_s, recv_s,
 ):
     R, W, C, nr, nc = sizes
     n = nr * nc
     q = W // R
-    group, owners = split_of(n)
+    group, owners = GROUP, OWNERS
+    bins = head_t.shape[0]
+    extent = R * nr
     row = lax.axis_index("row")
     col = lax.axis_index("col")
     me = row * nc + col
@@ -114,8 +115,6 @@
         return ref[pl.ds(r, 8), pl.ds(c, cols), :].astype(BF16).reshape(8 * cols, C)
 
     taps = [(a, b) for a in (-1, 0, 1) for b in (-1, 0, 1)]
-    inv_count = par[4:5, :]
-
     barrier = pltpu.get_barrier_semaphore()
 
     def greet(k, carry):
@@ -126,11 +125,37 @@
     h2[...] = jnp.zeros_like(h2)
     du[...] = jnp.zeros_like(du)
     lax.fori_loop(1, n, greet, 0)
+
+    def fill_row(i, carry):
+        at = row * R + i - 4
+        there = (at >= 0) & (at < extent)
+        value = jnp.where(there, mask_s[jnp.clip(at, 0, extent - 1)], 0).astype(F32)
+        rowm[i] = jnp.full((1, LANES), value, F32)
+        return carry
+
+    lax.fori_loop(0, R + 8, fill_row, 0)
+    spread = jnp.broadcast_to(mask_v[...].astype(F32), (LANES, extent)).T
+    colall[0:8, :] = jnp.zeros((8, LANES), F32)
+    colall[8 : 8 + extent, :] = spread
+    colall[8 + extent : 16 + extent, :] = jnp.zeros((8, LANES), F32)
+    colm[...] = colall[pl.ds(pl.multiple_of(col * W, 8), W + 16), :]
+    valid = jnp.sum(spread, axis=0, keepdims=True)
+    inv_wide = 1.0 / (valid * valid)
+    inv_count = inv_wide[:, :C]
     pl.semaphore_wait(barrier, n - 1)
 
     pair_spec = (0, pair, (0, 0), pb, (8, 16), (8, 16))
     halo_start(*pair_spec)
     pb[8 : 8 + R, 16 : 16 + W, :] = pair[...]
+    hwf[...] = jnp.zeros_like(hwf)
+    hwf[0:bins, :] = head_t[...].astype(F32)
+    hb[...] = jnp.full((1, LANES), -1e30, F32)
+    hb[:, 0:bins] = bias_in[...]
+    wide = hwf[...]
+    hw[...] = wide.astype(BF16)
+    none = jnp.zeros((LANES, C), F32)
+    hw2[0:LANES, :] = jnp.concatenate([wide, none], axis=1).astype(BF16)
+    hw2[LANES : 2 * LANES, :] = jnp.concatenate([none, wide], axis=1).astype(BF16)
     halo_recv(*pair_spec)
     pf[...] = pb[...].astype(F32)
 
@@ -171,9 +196,15 @@
         return mean, 1.0 / jnp.sqrt(var + EPSILON)
 
     moments(h1, st1, 0)
+
+    def spread_labels(r, carry):
+        lab[r] = jnp.broadcast_to(labels[pl.ds(r, 1), :].astype(F32), (LANES, W)).T
+        return carry
+
+    lax.fori_loop(0, R, spread_labels, 0)
     mean1, inv1 = mean_inverse(gathered(st1, 0))
-    scale1 = par[0:1, :] * inv1
-    shift1 = par[1:2, :] - mean1 * scale1
+    scale1 = gain[0:1, :] * inv1
+    shift1 = shift[0:1, :] - mean1 * scale1
 
     def first_act(r):
         v = h1[pl.ds(r, 8)] * scale1[None] + shift1[None]
@@ -195,34 +226,35 @@
     h2_spec = (1, h2, (4, 8), h2, (4, 8), (4, 8))
     halo_start(*h2_spec)
     mean2, inv2 = mean_inverse(gathered(st2, 1))
-    gain2 = par[2:3, :]
+    gain2 = gain[1:2, :]
 
     def features(r):
         xhat = (h2[pl.ds(4 + r, 8), 8 : 8 + W, :] - mean2[None]) * inv2[None]
-        u = gain2[None] * xhat + par[3:4, :][None] + pf[pl.ds(8 + r, 8), 16 : 16 + W, :]
+        u = gain2[None] * xhat + shift[1:2, :][None] + pf[pl.ds(8 + r, 8), 16 : 16 + W, :]
         return xhat, u
 
     def head(r):
         _, u = features(r)
-        y = (pmask(r, C) * elu(u)).astype(BF16).reshape(8 * W, C)
-        z = jnp.dot(y, hw[...], preferred_element_type=F32) + hb[...]
-        yb[pl.ds(r, 8)] = y.reshape(8, W, C)
-        zb[pl.ds(r, 8)] = z.reshape(8, W, LANES)
+        yf[pl.ds(r, 8)] = (pmask(r, C) * elu(u)).astype(BF16).astype(F32)
 
     blocks(R // 8, head)
 
+    half = R // 2
     has_self = row // q == col
     mine = row % q
 
     def mirror_copy(b):
         return pltpu.make_async_remote_copy(
-            src_ref=zb.at[:, pl.ds(b * R, R), :], dst_ref=zr.at[mine],
+            src_ref=yp.at[b], dst_ref=yr.at[mine],
             send_sem=send_s.at[2], recv_sem=recv_s.at[2],
             device_id=(col * q + b, row // q), device_id_type=MESH,
         )
 
     for b in range(q):
         stays = has_self & (mine == b)
+        block = yf[:, b * R : (b + 1) * R, :]
+        packed = jnp.concatenate([block[:half], block[half:]], axis=2)
+        yp[b] = packed.reshape(half * R, LANES).astype(BF16)
 
         @pl.when(jnp.logical_not(stays))
         def _():
@@ -230,32 +262,46 @@
 
         @pl.when(stays)
         def _():
-            zr[b] = zb[:, b * R : (b + 1) * R, :]
+            yr[b] = yp[b]
+
+    def logits(r):
+        y = yf[pl.ds(r, 8)].astype(BF16).reshape(8 * W, C)
+        z = lax.dot_general(y, hw[...], NT, preferred_element_type=F32) + hb[...]
+        zb[pl.ds(r, 8)] = z.reshape(8, W, LANES)
+
+    blocks(R // 8, logits)
 
     @pl.when(has_self)
     def _():
-        wait_bytes(zr.at[pl.ds(0, q - 1)], recv_s.at[2])
+        wait_bytes(yr.at[pl.ds(0, q - 1)], recv_s.at[2])
 
     @pl.when(jnp.logical_not(has_self))
     def _():
-        wait_bytes(zr, recv_s.at[2])
-
+        wait_bytes(yr, recv_s.at[2])
+
+    zz[...] = lax.dot_general(
+        yr[...].reshape(q * half * R, LANES), hw2[...], NT, preferred_element_type=F32
+    )
     for b in range(q):
-        zt[:, b * R : (b + 1) * R, :] = jnp.swapaxes(zr[b], 0, 1)
+        z = zz[b * half * R : (b + 1) * half * R, :]
+        low = z[:, :LANES].reshape(half, R, LANES)
+        high = z[:, LANES:].reshape(half, R, LANES)
+        whole = jnp.concatenate([low, high], axis=0) + hb[...][None]
+        zt[:, b * R : (b + 1) * R, :] = jnp.swapaxes(whole, 0, 1)
 
     def loss_part(first, r):
         s = 0.5 * (zb[pl.ds(r, 8)] + zt[pl.ds(r, 8)])
         top = jnp.max(s, axis=2, keepdims=True)
         log_total = top + jnp.log(jnp.sum(jnp.exp(s - top), axis=2, keepdims=True))
-        bins = lax.broadcasted_iota(jnp.int32, (8, W, LANES), 2)
-        hot = bins == lab[pl.ds(r, 8)]
+        bin_of = lax.broadcasted_iota(jnp.int32, (8, W, LANES), 2).astype(F32)
+        hot = bin_of == lab[pl.ds(r, 8)]
         m = pmask(r, LANES)
         lossy = m * jnp.where(hot, log_total - s, 0.0)
         g = m * (jnp.exp(s - log_total) - jnp.where(hot, 1.0, 0.0))
         gh = g.astype(BF16).reshape(8 * W, LANES)
-        y = yb[pl.ds(r, 8)].reshape(8 * W, C)
-        head_part = jnp.dot(y.astype(F32).T.astype(BF16), gh, preferred_element_type=F32)
-        dy = lax.dot_general(gh, hw[...], NT, preferred_element_type=F32).reshape(8, W, C)
+        y = yf[pl.ds(r, 8)].reshape(8 * W, C)
+        head_part = jnp.dot(y.T.astype(BF16), gh, preferred_element_type=F32)
+        dy = jnp.dot(gh, hw[...], preferred_element_type=F32).reshape(8, W, C)
         xhat, u = features(r)
         grad = dy * pmask(r, C) * jnp.where(u > 0, 1.0, jnp.exp(jnp.minimum(u, 0.0)))
         du[pl.ds(4 + r, 8), 8 : 8 + W, :] = grad
@@ -286,7 +332,10 @@
     halo_recv(*h2_spec)
     halo_recv(*du_spec)
     sums3 = gathered(st3, 3)
-    tail_out[...] = sums3
+    bias_out[...] = sums3[1:2, :bins] / extent
+    norm_out[0:1, :] = sums3[0:1, :C] / extent
+    norm_out[1:2, :] = sums3[0:1, C:] / extent
+    loss_out[...] = jnp.sum(sums3[2:3, :], axis=1, keepdims=True) * inv_wide[:, 0:1]
     scale_mean = sums3[0:1, :C] * inv_count
     shift_mean = sums3[0:1, C:] * inv_count
     back = gain2 * inv2
@@ -352,16 +401,23 @@
     @pl.when(is_owner)
     def _():
         wait_bytes(gath.at[pl.ds(0, n - 1)], recv_s.at[4])
-        red[pl.ds(my_owner * group, group)] = jnp.sum(gath[...], axis=0)
-        mine_red = red.at[pl.ds(my_owner * group, group)]
-        to_all((mine_red, send_s.at[5], recv_s.at[5]))
-        wait_bytes(red.at[pl.ds(0, (owners - 1) * group)], recv_s.at[5])
+        total = jnp.sum(gath[...], axis=0).reshape(8 * group, LANES)
+        red[my_owner] = total.astype(BF16)
+        to_all((red.at[my_owner], send_s.at[5], recv_s.at[5]))
+        wait_bytes(red.at[pl.ds(0, owners - 1)], recv_s.at[5])
 
     @pl.when(jnp.logical_not(is_owner))
     def _():
         wait_bytes(red, recv_s.at[5])
 
-    gsum_out[...] = red[...]
+    sums = red[...].astype(F32) * (1.0 / extent)
+    for k in range(5):
+        pair_of = sums[4 * k : 4 * k + 4].reshape(C, LANES)
+        grads_out[2 * k] = pair_of[:, :C]
+        if k < 4:
+            grads_out[2 * k + 1] = pair_of[:, C:]
+        else:
+            head_out[...] = pair_of[:, C:].T[:bins, :]
 
     halo_sent(*pair_spec)
     halo_sent(*h2_spec)
@@ -372,16 +428,16 @@
 
     @pl.when(has_self)
     def _():
-        wait_bytes(zr.at[pl.ds(0, q - 1)], send_s.at[2])
+        wait_bytes(yp.at[pl.ds(0, q - 1)], send_s.at[2])
 
     @pl.when(jnp.logical_not(has_self))
     def _():
-        wait_bytes(zr, send_s.at[2])
+        wait_bytes(yp, send_s.at[2])
 
     @pl.when(is_owner)
     def _():
         wait_bytes(part.at[pl.ds(0, (owners - 1) * group)], send_s.at[4])
-        wait_bytes(gath.at[pl.ds(0, n - 1)], send_s.at[5])
+        wait_bytes(gath.at[pl.ds(0, n - 1), pl.ds(0, 1)], send_s.at[5])
 
     @pl.when(jnp.logical_not(is_owner))
     def _():
@@ -396,37 +452,30 @@
     K = head_weight.shape[1]
     nr, nc = lax.axis_size("row"), lax.axis_size("col")
     n = nr * nc
-    group, owners = split_of(n)
-    extent = R * nr
-    mask_float = mask.astype(F32)
-    valid = jnp.sum(mask_float)
-    count = valid * valid
-    padded = jnp.pad(mask_float, (8, 8))
-    rows = lax.dynamic_slice_in_dim(padded, lax.axis_index("row") * R + 4, R + 8)
-    cols = lax.dynamic_slice_in_dim(padded, lax.axis_index("col") * W, W + 16)
-    rowm = jnp.broadcast_to(rows[:, None, None], (R + 8, 1, LANES))
-    colm = jnp.broadcast_to(cols[:, None], (W + 16, LANES))
-    par = jnp.concatenate(
-        [
-            jnp.stack([norm_gain[0], norm_shift[0], norm_gain[1], norm_shift[1]]),
-            jnp.broadcast_to(1.0 / count, (4, C)),
-        ]
-    )
-    hw = jnp.pad(head_weight, ((0, 0), (0, LANES - K)))
-    hb = jnp.pad(head_bias[None], ((0, 0), (0, LANES - K)), constant_values=-1e30)
     vmem = pl.BlockSpec(memory_space=pltpu.VMEM)
     smem = pl.BlockSpec(memory_space=pltpu.SMEM)
     ring = (R + 8, W + 16, C)
-    act, gsum, tail = pl.pallas_call(
+    act, grads, head, bias, norm, loss = pl.pallas_call(
         functools.partial(kernel, (R, W, C, nr, nc)),
         out_shape=(
             jax.ShapeDtypeStruct((R, W, C), BF16),
-            jax.ShapeDtypeStruct((40, 8, LANES), F32),
-            jax.ShapeDtypeStruct((4, LANES), F32),
+            jax.ShapeDtypeStruct((9, C, C), F32),
+            jax.ShapeDtypeStruct((K, C), F32),
+            jax.ShapeDtypeStruct((1, K), F32),
+            jax.ShapeDtypeStruct((2, C), F32),
+            jax.ShapeDtypeStruct((1, 1), F32),
         ),
-        in_specs=[smem] + [vmem] * 9,
-        out_specs=(vmem, vmem, vmem),
+        in_specs=[smem, smem] + [vmem] * 9,
+        out_specs=(vmem,) * 6,
         scratch_shapes=[
+            pltpu.VMEM((R + 8, 1, LANES), F32),
+            pltpu.VMEM((W + 16, LANES), F32),
+            pltpu.VMEM((R * nr + 16, LANES), F32),
+            pltpu.VMEM((R, W, LANES), F32),
+            pltpu.VMEM((LANES, C), F32),
+            pltpu.VMEM((LANES, C), BF16),
+            pltpu.VMEM((2 * LANES, LANES), BF16),
+            pltpu.VMEM((1, LANES), F32),
             pltpu.VMEM((R + 16, W + 32, C), BF16),
             pltpu.VMEM((R + 16, W + 32, C), F32),
             pltpu.VMEM(ring, F32),
@@ -434,16 +483,18 @@
             pltpu.VMEM(ring, F32),
             pltpu.VMEM(ring, F32),
             pltpu.VMEM(ring, F32),
-            pltpu.VMEM((R, W, C), BF16),
+            pltpu.VMEM((R, W, C), F32),
             pltpu.VMEM((R, W, LANES), F32),
-            pltpu.VMEM((W // R, R, R, LANES), F32),
+            pltpu.VMEM((W // R, R * R // 2, LANES), BF16),
+            pltpu.VMEM((W // R, R * R // 2, LANES), BF16),
+            pltpu.VMEM((W * R // 2, 2 * LANES), F32),
             pltpu.VMEM((R, W, LANES), F32),
             pltpu.VMEM((n, 1, LANES), F32),
             pltpu.VMEM((n, 1, LANES), F32),
             pltpu.VMEM((n, 4, LANES), F32),
             pltpu.VMEM((40, 8, LANES), F32),
-            pltpu.VMEM((n, group, 8, LANES), F32),
-            pltpu.VMEM((40, 8, LANES), F32),
+            pltpu.VMEM((n, GROUP, 8, LANES), F32),
+            pltpu.VMEM((OWNERS, 8 * GROUP, LANES), BF16),
             pltpu.SemaphoreType.DMA((3, 8)),
             pltpu.SemaphoreType.DMA((3, 8)),
             pltpu.SemaphoreType.DMA((6,)),
@@ -453,18 +504,10 @@
             collective_id=0, has_side_effects=True, vmem_limit_bytes=56 * 1024 * 1024
         ),
     )(
-        dilations, pair.transpose(1, 2, 0), rowm, colm, labels[:, :, None],
-        conv_first, conv_second, par, hw, hb,
+        dilations, mask, mask[None], pair.transpose(1, 2, 0), labels,
+        conv_first, conv_second, norm_gain, norm_shift, head_weight.T, head_bias[None],
     )
-    grads = gsum.reshape(5, C, 2, C).transpose(0, 2, 1, 3).reshape(10, C, C) / extent
-    return (
-        jnp.sum(tail[2]) / count,
-        grads[9][:, :K],
-        tail[1, :K] / extent,
-        tail[0].reshape(2, C) / extent,
-        grads[:9],
-        act.transpose(2, 0, 1),
-    )
+    return loss[0, 0], head.T, bias[0], norm, grads, act.transpose(2, 0, 1)
 
 
 def solution(mesh):

time: 76.4 us -> 59.8 us (0.78)
  Pallas kernels: 57.5 us -> 50.4 us
  other arithmetic: 4.04 us -> 0 us
  local copies, waits for them, and re-layouts: 10.2 us -> 6.71 us
  between operations: 3.84 us -> 2.43 us
    pallas_call x1, Pallas kernels: 57.5 us -> 50.4 us  [body(): pl.pallas_call(functools.partial(kernel, (R, W, C, nr, nc)), out_shape=(j...]
    unnamed x12, local copies, waits for them, and re-layouts: 3.09 us -> 6.71 us
    broadcast_in_dim x4 -> x0, local copies, waits for them, and re-layouts: 2.23 us -> none  [the longest x1 0.86 us: body(): labels[:, :, None]]
    div x3 -> x0, other arithmetic: 2.08 us -> none  [the longest x1 0.96 us: body(): gsum.reshape(5, C, 2, C).transpose(0, 2, 1, 3).reshape(10, C, C) / extent]
    pad x2 -> x0, local copies, waits for them, and re-layouts: 1.78 us -> none  [the longest x1 1.17 us: body(): jnp.pad(head_bias[None], ((0, 0), (0, LANES - K)), constant_values=-1e+30)]
    slice x2 -> x0, local copies, waits for them, and re-layouts: 1.5 us -> none  [the longest x1 0.76 us: body(): norm_shift[1]]
    reduce_sum x1 -> x0, other arithmetic: 1.3 us -> none  [body(): valid = jnp.sum(mask_float)]
    div x3 -> x0, local copies, waits for them, and re-layouts: 0.88 us -> none  [the longest x1 0.64 us: body(): tail[0].reshape(2, C) / extent]
where the time goes in v2:
time: 59.8 us; the launch traced here: 59.5 us
  Pallas kernels  50.4 us (84%)
  local copies, waits for them, and re-layouts  6.71 us (11%)
  between operations  2.43 us (4%)
    pallas_call x1, Pallas kernels, body(): pl.pallas_call(functools.partial(kernel, (R, W, C, nr, nc)), out_shape=(j...  50.4 us
    unnamed x12, local copies, waits for them, and re-layouts  6.71 us

profile of v2, /device:TPU:0, one launch (start us, length us, event | category | flops | bytes accessed | tf_op | source)
XLA Modules:
  0.0 59.5 jit_solution(10653002593057999366)
XLA Ops:
  0.6 1.7 %copy.16 = bf16[64,8,64]{0,2,1:T(8,128)(2,1)} copy(bf16[64,8,64]{2,1,0:T(8,128)(2,1)} %param.10) | data formatting | bytes 131072 | tf_op args[0]
  2.3 50.4 %shard_map.145 = (bf16[8,64,64]{2,1,0:T(8,128)(2,1)}, f32[9,64,64]{2,1,0:T(8,128)}, f32[37,64]{1,0:T(8,128)}, f32[1,37]{1,0:T(1,128)}, f32[2,64]{1,0:T(2,128)}, /*index=5*/f32[1,1]{1,0:T(1,128)}) custom-call(s32[2]{0:T(128)} %dil.1, s32[128]{0:T(128)} %mask_s.1, s32[1,128]{1,0:T(1,128)} %bitcast.12, bf16[8,64,64]{2,1,0:T(8,128)(2,1)} %bitcast.8, ...), custom_call_target="tpu_custom_call" | custom-call | tf_op jit(solution)/shard_map/pallas_call | solution.py:458
  52.7 0.0 copy-start
  52.7 1.7 %copy.17 = bf16[64,8,64]{2,1,0:T(8,128)(2,1)} copy(bf16[64,8,64]{0,2,1:T(8,128)(2,1)} %bitcast.9) | data formatting | bytes 131072
  55.1 0.0 copy-start.2
  55.1 1.3 %copy.24 = f32[64,37]{0,1:T(8,128)} copy(f32[64,37]{0,1:T(8,128)} %bitcast.10) | data formatting | bytes 18944
  56.4 0.0 copy-done.2
  56.4 0.0 copy-start.1
  56.4 0.5 copy.25
  57.0 0.2 copy-done.1
  57.1 0.6 copy.26
  57.7 0.0 copy-done
  57.7 0.7 %copy.27 = f32[9,64,64]{2,1,0:T(8,128)} copy(f32[9,64,64]{2,1,0:T(8,128)S(1)} %copy-done) | data formatting | bytes 294912
Async XLA Ops:
  52.7 5.0 %copy-start = (f32[9,64,64]{2,1,0:T(8,128)S(1)}, f32[9,64,64]{2,1,0:T(8,128)}, u32[]{:S(2)}) copy-start(f32[9,64,64]{2,1,0:T(8,128)} %get-tuple-element.34) | copy-start | bytes 442372
  55.1 1.3 %copy-start.2 = (f32[1,37]{1,0:T(1,128)S(1)}, f32[1,37]{1,0:T(1,128)}, u32[]{:S(2)}) copy-start(f32[1,37]{1,0:T(1,128)} %get-tuple-element.14) | copy-start | bytes 448
  56.4 0.7 %copy-start.1 = (f32[2,64]{1,0:T(2,128)S(1)}, f32[2,64]{1,0:T(2,128)}, u32[]{:S(2)}) copy-start(f32[2,64]{1,0:T(2,128)} %get-tuple-element.33) | copy-start | bytes 1540

commit v3 on v2

--- a/solution.py
+++ b/solution.py
@@ -27,7 +27,7 @@
     sizes, dil, mask_s, mask_v, pair, labels, w1, w2, gain, shift, head_t, bias_in,
     act_out, grads_out, head_out, bias_out, norm_out, loss_out,
     rowm, colm, colall, lab, hwf, hw, hw2, hb,
-    pb, pf, h1, a1, h2, du, dh, yf, zb, yp, yr, zz, zt, st1, st2, st3, part, gath, red,
+    pb, pf, h1, a1, h2, du, dh, yf, zb, yp, yr, zz, zt, st1, st2, st3, part, sent, gath, red,
     halo_s, halo_r, send_s, recv_s,
 ):
     R, W, C, nr, nc = sizes
@@ -43,17 +43,17 @@
     is_owner = jnp.logical_and(my_owner < owners, (my_owner * n) // owners == me)
 
     def device(p):
-        return (p // nc, p % nc)
+        return (lax.div(p, nc), lax.rem(p, nc))
 
     def to_all(slots):
         def step(k, carry):
             pltpu.make_async_remote_copy(
                 src_ref=slots[0], dst_ref=slots[0], send_sem=slots[1], recv_sem=slots[2],
-                device_id=device((me + k) % n), device_id_type=MESH,
+                device_id=device(lax.rem(me + k, n)), device_id_type=MESH,
             ).start()
             return carry
 
-        lax.fori_loop(1, n, step, 0)
+        lax.fori_loop(1, n, step, 0, unroll=4)
 
     def wait_bytes(ref, sem):
         pltpu.make_async_copy(ref, ref, sem).wait()
@@ -118,7 +118,7 @@
     barrier = pltpu.get_barrier_semaphore()
 
     def greet(k, carry):
-        pl.semaphore_signal(barrier, inc=1, device_id=device((me + k) % n), device_id_type=MESH)
+        pl.semaphore_signal(barrier, inc=1, device_id=device(lax.rem(me + k, n)), device_id_type=MESH)
         return carry
 
     pb[...] = jnp.zeros_like(pb)
@@ -369,20 +369,22 @@
             1, R // 8, lambda k, z: (weight_grad(False, pl.multiple_of(k * 8, 8)), z)[1], 0
         )
 
+    sent[...] = part[...].reshape(owners, 8 * group, LANES).astype(BF16)
+
     def scatter(k, carry):
-        target = (k * n) // owners
+        target = lax.div(k * n, owners)
 
         @pl.when(target != me)
         def _():
             pltpu.make_async_remote_copy(
-                src_ref=part.at[pl.ds(k * group, group)], dst_ref=gath.at[me],
+                src_ref=sent.at[k], dst_ref=gath.at[me],
                 send_sem=send_s.at[4], recv_sem=recv_s.at[4],
                 device_id=device(target), device_id_type=MESH,
             ).start()
 
         @pl.when(target == me)
         def _():
-            gath[me] = part[pl.ds(k * group, group)]
+            gath[me] = sent[k]
 
         return carry
 
@@ -401,7 +403,7 @@
     @pl.when(is_owner)
     def _():
         wait_bytes(gath.at[pl.ds(0, n - 1)], recv_s.at[4])
-        total = jnp.sum(gath[...], axis=0).reshape(8 * group, LANES)
+        total = jnp.sum(gath[...].astype(F32), axis=0)
         red[my_owner] = total.astype(BF16)
         to_all((red.at[my_owner], send_s.at[5], recv_s.at[5]))
         wait_bytes(red.at[pl.ds(0, owners - 1)], recv_s.at[5])
@@ -411,13 +413,8 @@
         wait_bytes(red, recv_s.at[5])
 
     sums = red[...].astype(F32) * (1.0 / extent)
-    for k in range(5):
-        pair_of = sums[4 * k : 4 * k + 4].reshape(C, LANES)
-        grads_out[2 * k] = pair_of[:, :C]
-        if k < 4:
-            grads_out[2 * k + 1] = pair_of[:, C:]
-        else:
-            head_out[...] = pair_of[:, C:].T[:bins, :]
+    grads_out[...] = sums.reshape(5, C, LANES)
+    head_out[...] = sums[16:20].reshape(C, LANES)[:, C:].T[:bins, :]
 
     halo_sent(*pair_spec)
     halo_sent(*h2_spec)
@@ -436,12 +433,12 @@
 
     @pl.when(is_owner)
     def _():
-        wait_bytes(part.at[pl.ds(0, (owners - 1) * group)], send_s.at[4])
-        wait_bytes(gath.at[pl.ds(0, n - 1), pl.ds(0, 1)], send_s.at[5])
+        wait_bytes(sent.at[pl.ds(0, owners - 1)], send_s.at[4])
+        wait_bytes(gath.at[pl.ds(0, n - 1)], send_s.at[5])
 
     @pl.when(jnp.logical_not(is_owner))
     def _():
-        wait_bytes(part, send_s.at[4])
+        wait_bytes(sent, send_s.at[4])
 
 
 def body(
@@ -459,7 +456,7 @@
         functools.partial(kernel, (R, W, C, nr, nc)),
         out_shape=(
             jax.ShapeDtypeStruct((R, W, C), BF16),
-            jax.ShapeDtypeStruct((9, C, C), F32),
+            jax.ShapeDtypeStruct((5, C, LANES), F32),
             jax.ShapeDtypeStruct((K, C), F32),
             jax.ShapeDtypeStruct((1, K), F32),
             jax.ShapeDtypeStruct((2, C), F32),
@@ -493,7 +490,8 @@
             pltpu.VMEM((n, 1, LANES), F32),
             pltpu.VMEM((n, 4, LANES), F32),
             pltpu.VMEM((40, 8, LANES), F32),
-            pltpu.VMEM((n, GROUP, 8, LANES), F32),
+            pltpu.VMEM((OWNERS, 8 * GROUP, LANES), BF16),
+            pltpu.VMEM((n, 8 * GROUP, LANES), BF16),
             pltpu.VMEM((OWNERS, 8 * GROUP, LANES), BF16),
             pltpu.SemaphoreType.DMA((3, 8)),
             pltpu.SemaphoreType.DMA((3, 8)),
@@ -507,6 +505,7 @@
         dilations, mask, mask[None], pair.transpose(1, 2, 0), labels,
         conv_first, conv_second, norm_gain, norm_shift, head_weight.T, head_bias[None],
     )
+    grads = grads.reshape(5, C, 2, C).transpose(0, 2, 1, 3).reshape(10, C, C)[:9]
     return loss[0, 0], head.T, bias[0], norm, grads, act.transpose(2, 0, 1)
 
 

time: 59.8 us -> 56.6 us (0.946)
  Pallas kernels: 50.4 us -> 47.8 us
  local copies, waits for them, and re-layouts: 6.71 us -> 6.1 us
    pallas_call x1, Pallas kernels: 50.4 us -> 47.8 us  [body(): pl.pallas_call(functools.partial(kernel, (R, W, C, nr, nc)), out_shape=(j...]
    unnamed x12 -> x13, local copies, waits for them, and re-layouts: 6.71 us -> 5.27 us
    slice x0 -> x2, local copies, waits for them, and re-layouts: none -> 0.83 us  [the longest x1 0.74 us: body(): grads.reshape(5, C, 2, C).transpose(0, 2, 1, 3).reshape(10, C, C)[:9]]
where the time goes in v3:
time: 56.6 us; the launch traced here: 56.4 us
  Pallas kernels  47.8 us (84%)
  local copies, waits for them, and re-layouts  6.1 us (11%)
  between operations  2.5 us (4%)
    pallas_call x1, Pallas kernels, body(): pl.pallas_call(functools.partial(kernel, (R, W, C, nr, nc)), out_shape=(j...  47.8 us
    unnamed x13, local copies, waits for them, and re-layouts  5.27 us

profile of v3, /device:TPU:0, one launch (start us, length us, event | category | flops | bytes accessed | tf_op | source)
XLA Modules:
  0.0 56.4 jit_solution(11195292846146391459)
XLA Ops:
  0.6 1.7 %copy.16 = bf16[64,8,64]{0,2,1:T(8,128)(2,1)} copy(bf16[64,8,64]{2,1,0:T(8,128)(2,1)} %param.10) | data formatting | bytes 131072 | tf_op args[0]
  2.3 47.8 %shard_map.145 = (bf16[8,64,64]{2,1,0:T(8,128)(2,1)}, f32[5,64,128]{2,1,0:T(8,128)}, f32[37,64]{1,0:T(8,128)}, f32[1,37]{1,0:T(1,128)}, f32[2,64]{1,0:T(2,128)}, /*index=5*/f32[1,1]{1,0:T(1,128)}) custom-call(s32[2]{0:T(128)} %dil.1, s32[128]{0:T(128)} %mask_s.1, s32[1,128]{1,0:T(1,128)} %bitcast.14, bf16[8,64,64]{2,1,0:T(8,128)(2,1)} %bitcast.10, ...), custom_call_target="tpu_custom_call" | custom-call | tf_op jit(solution)/shard_map/pallas_call | solution.py:455
  50.1 0.0 copy-start
  50.1 1.7 %copy.17 = bf16[64,8,64]{2,1,0:T(8,128)(2,1)} copy(bf16[64,8,64]{0,2,1:T(8,128)(2,1)} %bitcast.11) | data formatting | bytes 131072
  51.8 0.0 copy-done
  51.8 0.1 fusion
  51.9 0.0 copy-start.1
  52.0 0.7 %slice.12 = f32[9,64,64]{2,1,0:T(8,128)} slice(f32[10,64,64]{2,1,0:T(8,128)S(1)} %bitcast.9), slice={[0:9], [0:64], [0:64]} | slice | bytes 294912 | tf_op jit(solution)/shard_map/slice | solution.py:508
  53.4 0.0 copy-done.1
  53.4 0.0 copy-start.3
  53.4 0.6 %copy.23 = f32[64,37]{0,1:T(8,128)} copy(f32[64,37]{0,1:T(8,128)S(1)} %bitcast.12) | data formatting | bytes 18944
  54.0 0.0 copy-done.3
  54.0 0.0 copy-start.2
  54.0 0.5 copy.24
  54.5 0.2 copy-done.2
  54.7 0.6 copy.25
  (1 shorter events, 0.0 us)
Async XLA Ops:
  50.1 1.7 %copy-start = (f32[5,64,128]{2,1,0:T(8,128)S(1)}, f32[5,64,128]{2,1,0:T(8,128)}, u32[]{:S(2)}) copy-start(f32[5,64,128]{2,1,0:T(8,128)} %get-tuple-element.16) | copy-start | bytes 491524
  51.9 1.4 %copy-start.1 = (f32[37,64]{1,0:T(8,128)S(1)}, f32[37,64]{1,0:T(8,128)}, u32[]{:S(2)}) copy-start(f32[37,64]{1,0:T(8,128)} %get-tuple-element.13) | copy-start | bytes 28420
  53.4 0.6 %copy-start.3 = (f32[1,37]{1,0:T(1,128)S(1)}, f32[1,37]{1,0:T(1,128)}, u32[]{:S(2)}) copy-start(f32[1,37]{1,0:T(1,128)} %get-tuple-element.14) | copy-start | bytes 448
  54.0 0.7 %copy-start.2 = (f32[2,64]{1,0:T(2,128)S(1)}, f32[2,64]{1,0:T(2,128)}, u32[]{:S(2)}) copy-start(f32[2,64]{1,0:T(2,128)} %get-tuple-element.35) | copy-start | bytes 1540

commit v4 on v3

--- a/solution.py
+++ b/solution.py
@@ -24,9 +24,9 @@
 
 
 def kernel(
-    sizes, dil, mask_s, mask_v, pair, labels, w1, w2, gain, shift, head_t, bias_in,
+    sizes, dil, mask_s, mask_v, pair_in, labels, w1, w2, gain, shift, head_t, bias_in,
     act_out, grads_out, head_out, bias_out, norm_out, loss_out,
-    rowm, colm, colall, lab, hwf, hw, hw2, hb,
+    pair, turned, ga, rowm, colm, colall, lab, hwf, hw, hw2, hb,
     pb, pf, h1, a1, h2, du, dh, yf, zb, yp, yr, zz, zt, st1, st2, st3, part, sent, gath, red,
     halo_s, halo_r, send_s, recv_s,
 ):
@@ -125,6 +125,10 @@
     h2[...] = jnp.zeros_like(h2)
     du[...] = jnp.zeros_like(du)
     lax.fori_loop(1, n, greet, 0)
+
+    turned[...] = pair_in[...].astype(F32)
+    for r in range(R):
+        pair[r] = turned[:, r, :].T.astype(BF16)
 
     def fill_row(i, carry):
         at = row * R + i - 4
@@ -396,9 +400,12 @@
             x = window(dh, r + 4 - a * d1, 8 - b * d1, W)
             term = jnp.dot(x, w2[t], preferred_element_type=F32)
             total = term if total is None else total + term
-        act_out[pl.ds(r, 8)] = total.reshape(8, W, C).astype(BF16)
+        ga[pl.ds(r, 8)] = total.reshape(8, W, C)
 
     blocks(R // 8, input_grad)
+    for r in range(R):
+        turned[:, r, :] = ga[r].T
+    act_out[...] = turned[...].astype(BF16)
 
     @pl.when(is_owner)
     def _():
@@ -455,7 +462,7 @@
     act, grads, head, bias, norm, loss = pl.pallas_call(
         functools.partial(kernel, (R, W, C, nr, nc)),
         out_shape=(
-            jax.ShapeDtypeStruct((R, W, C), BF16),
+            jax.ShapeDtypeStruct((C, R, W), BF16),
             jax.ShapeDtypeStruct((5, C, LANES), F32),
             jax.ShapeDtypeStruct((K, C), F32),
             jax.ShapeDtypeStruct((1, K), F32),
@@ -465,6 +472,9 @@
         in_specs=[smem, smem] + [vmem] * 9,
         out_specs=(vmem,) * 6,
         scratch_shapes=[
+            pltpu.VMEM((R, W, C), BF16),
+            pltpu.VMEM((C, R, W), F32),
+            pltpu.VMEM((R, W, C), F32),
             pltpu.VMEM((R + 8, 1, LANES), F32),
             pltpu.VMEM((W + 16, LANES), F32),
             pltpu.VMEM((R * nr + 16, LANES), F32),
@@ -502,11 +512,11 @@
             collective_id=0, has_side_effects=True, vmem_limit_bytes=56 * 1024 * 1024
         ),
     )(
-        dilations, mask, mask[None], pair.transpose(1, 2, 0), labels,
+        dilations, mask, mask[None], pair, labels,
         conv_first, conv_second, norm_gain, norm_shift, head_weight.T, head_bias[None],
     )
     grads = grads.reshape(5, C, 2, C).transpose(0, 2, 1, 3).reshape(10, C, C)[:9]
-    return loss[0, 0], head.T, bias[0], norm, grads, act.transpose(2, 0, 1)
+    return loss[0, 0], head.T, bias[0], norm, grads, act
 
 
 def solution(mesh):

time: 56.6 us -> 54.9 us (0.970)
  local copies, waits for them, and re-layouts: 6.1 us -> 4.35 us
    unnamed x13 -> x12, local copies, waits for them, and re-layouts: 5.27 us -> 2.52 us
    slice x1, local copies, waits for them, and re-layouts: 0.1 us -> 1.09 us
where the time goes in v4:
time: 54.9 us; the launch traced here: 54.7 us
  Pallas kernels  47.8 us (87%)
  local copies, waits for them, and re-layouts  4.35 us (8%)
  between operations  2.5 us (5%)
    pallas_call x1, Pallas kernels, body(): pl.pallas_call(functools.partial(kernel, (R, W, C, nr, nc)), out_shape=(j...  47.8 us
    unnamed x12, local copies, waits for them, and re-layouts  2.52 us

profile of v4, /device:TPU:0, one launch (start us, length us, event | category | flops | bytes accessed | tf_op | source)
XLA Modules:
  0.0 54.7 jit_solution(2929346583925221630)
XLA Ops:
  0.6 47.8 %shard_map.145 = (bf16[64,8,64]{2,1,0:T(8,128)(2,1)}, f32[5,64,128]{2,1,0:T(8,128)}, f32[37,64]{1,0:T(8,128)}, f32[1,37]{1,0:T(1,128)}, f32[2,64]{1,0:T(2,128)}, /*index=5*/f32[1,1]{1,0:T(1,128)}) custom-call(s32[2]{0:T(128)} %dil.1, s32[128]{0:T(128)} %mask_s.1, s32[1,128]{1,0:T(1,128)} %bitcast.10, bf16[64,8,64]{2,1,0:T(8,128)(2,1)} %pair_in.1, ...), custom_call_target="tpu_custom_call" | custom-call | tf_op jit(solution)/shard_map/pallas_call | solution.py:462
  48.4 1.1 %fusion = (f32[5,64,64]{2,1,0:T(8,128)S(1)}, f32[5,64,64]{2,1,0:T(8,128)S(1)}) fusion(f32[5,64,128]{2,1,0:T(8,128)} %get-tuple-element.16), kind=kLoop, calls=%fused_computation.1 | loop fusion | bytes 327680 | tf_op jit(solution)/shard_map/slice
  49.6 0.0 copy-start.1
  49.6 0.0 copy-start
  49.6 0.7 %slice.12 = f32[9,64,64]{2,1,0:T(8,128)} slice(f32[10,64,64]{2,1,0:T(8,128)S(1)} %bitcast.7), slice={[0:9], [0:64], [0:64]} | slice | bytes 294912 | tf_op jit(solution)/shard_map/slice | solution.py:518
  51.0 0.0 copy-done.1
  51.0 0.0 copy-start.3
  51.0 0.6 %copy.22 = f32[64,37]{0,1:T(8,128)} copy(f32[64,37]{0,1:T(8,128)S(1)} %bitcast.8) | data formatting | bytes 18944
  51.6 0.0 copy-done.3
  51.6 0.0 copy-start.2
  51.6 0.5 copy.23
  52.2 0.2 copy-done.2
  52.3 0.6 %copy.24 = f32[2,64]{1,0:T(2,128)} copy(f32[2,64]{1,0:T(2,128)S(1)} %copy-done.2) | data formatting | bytes 1024
  52.9 0.0 copy-done
  52.9 0.7 %copy.25 = bf16[64,8,64]{2,1,0:T(8,128)(2,1)} copy(bf16[64,8,64]{2,1,0:T(8,128)(2,1)S(1)} %copy-done) | data formatting | bytes 131072
  (1 shorter events, 0.0 us)
Async XLA Ops:
  49.6 1.4 %copy-start.1 = (f32[37,64]{1,0:T(8,128)S(1)}, f32[37,64]{1,0:T(8,128)}, u32[]{:S(2)}) copy-start(f32[37,64]{1,0:T(8,128)} %get-tuple-element.13) | copy-start | bytes 28420
  49.6 3.3 %copy-start = (bf16[64,8,64]{2,1,0:T(8,128)(2,1)S(1)}, bf16[64,8,64]{2,1,0:T(8,128)(2,1)}, u32[]{:S(2)}) copy-start(bf16[64,8,64]{2,1,0:T(8,128)(2,1)} %get-tuple-element.31) | copy-start | bytes 196612
  51.0 0.6 %copy-start.3 = (f32[1,37]{1,0:T(1,128)S(1)}, f32[1,37]{1,0:T(1,128)}, u32[]{:S(2)}) copy-start(f32[1,37]{1,0:T(1,128)} %get-tuple-element.14) | copy-start | bytes 448
  51.6 0.7 %copy-start.2 = (f32[2,64]{1,0:T(2,128)S(1)}, f32[2,64]{1,0:T(2,128)}, u32[]{:S(2)}) copy-start(f32[2,64]{1,0:T(2,128)} %get-tuple-element.29) | copy-start | bytes 1540
